TPU v7x, 128 devices: a whole 4x4x4 slice. The times are simulated.
128 devices in a mesh: ctx: 8 (over z_lo, y), rec: 16 (over z_hi, x, core).
Axes of the slice: x: 4, y: 4, z: 4 (z_hi: 2, z_lo: 2; z = z_hi * 2 + z_lo), core: 2. Of those that a mesh axis runs over, the one named last changes fastest.
Arguments:
- layer_in: bfloat16 [16, 2048, 1024], P('rec', 'ctx'), may hold values from -6 to 6
- queries: bfloat16 [16, 2048, 1024], P('rec', 'ctx'), may hold values from -6 to 6, as said below
- keys: bfloat16 [16, 2048, 1024], P('rec', 'ctx'), may hold values from -6 to 6, as said below
- values: bfloat16 [16, 2048, 1024], P('rec', 'ctx'), may hold values from -6 to 6
- lengths: int32 [16], P('rec'), may hold values from 512 to 2048, as said below
- w_qkv: bfloat16 [1024, 3072], replicated, may hold values from -0.1875 to 0.1875
- w_out: bfloat16 [1024, 1024], replicated, may hold values from -0.1875 to 0.1875
- conv_kernel: float32 [9, 1024], replicated, may hold values from -2.5 to 2.5
- grad_out: bfloat16 [16, 2048, 1024], P('rec', 'ctx'), may hold values from -6 to 6
Outputs:
- d_input: bfloat16 [16, 2048, 1024], P('rec', 'ctx')
- d_w_qkv: float32 [1024, 3072], P(('ctx', 'rec'))
- d_w_out: float32 [1024, 1024], P(('ctx', 'rec'))
- d_kernel: float32 [9, 1024], replicated
Inputs may be any that keep to these rules, and one draw needn't show every extreme that they name: `queries`: entries of order one. `keys`: entries of order one. `lengths`: some recording has all 2048 frames valid.
All inputs are finite; a program needn't handle non-finite values.
Results may differ from a plain program's by a relative error of at most 0.013.
Values may be sent and summed in bfloat16 or wider, within the bound.
A program may use at most 128 MiB of HBM per device.

v0:
```python
import math

import jax
import jax.numpy as jnp
from jax import lax
from jax.sharding import PartitionSpec as P

HEAD_DIM = 128
KW = 9


def padded_2(block, sides, width):
    for axis, dim in sides:
        count = lax.axis_size(axis)
        forward = [(i, i + 1) for i in range(count - 1)]
        backward = [(target, source) for source, target in forward]
        low = lax.ppermute(
            lax.slice_in_dim(block, block.shape[dim] - width, None, axis=dim), axis, forward
        )
        high = lax.ppermute(lax.slice_in_dim(block, 0, width, axis=dim), axis, backward)
        block = jnp.concatenate([low, block, high], axis=dim)
    return block


def shards(layer_in, queries, keys, values, lengths, w_qkv, w_out, conv_kernel, grad_out):
    n_recs, frames, model_width = layer_in.shape
    n_heads = model_width // HEAD_DIM
    inv_root = 1.0 / math.sqrt(HEAD_DIM)
    reach = KW // 2

    def split_heads(tensor):
        return tensor.reshape(tensor.shape[0], tensor.shape[1], n_heads, HEAD_DIM)

    keys_all, values_all = (
        lax.all_gather(keys, "ctx", axis=1, tiled=True),
        lax.all_gather(values, "ctx", axis=1, tiled=True),
    )
    all_frames = keys_all.shape[1]
    q_heads = split_heads(queries)
    k_all = split_heads(keys_all)
    v_all = split_heads(values_all)
    valid = jnp.arange(all_frames)[None, :] < lengths[:, None]
    scores = (
        jnp.einsum("rihe,rjhe->rhij", q_heads, k_all, preferred_element_type=jnp.float32) * inv_root
    )
    scores = jnp.where(valid[:, None, None, :], scores, -jnp.inf)
    row_max = jnp.max(scores, axis=-1, keepdims=True)
    log_total = row_max + jnp.log(jnp.sum(jnp.exp(scores - row_max), axis=-1, keepdims=True))
    attn_probs = jnp.exp(scores - log_total).astype(jnp.bfloat16)
    attended = jnp.einsum("rhij,rjhe->rihe", attn_probs, v_all, preferred_element_type=jnp.float32)
    attended = attended.reshape(n_recs, frames, model_width).astype(jnp.bfloat16)
    sublayer = jnp.einsum(
        "rid,de->rie", attended, w_out, preferred_element_type=jnp.float32
    ).astype(jnp.bfloat16)
    padded = padded_2(jnp.stack([grad_out, sublayer]), (("ctx", 2),), reach)
    grad_pad = padded[0].astype(jnp.float32)
    sub_pad = padded[1].astype(jnp.float32)
    grad_f = grad_out.astype(jnp.float32)
    d_sub = grad_f
    kernel_rows = []
    for offset in range(KW):
        start = 2 * reach - offset
        d_sub = d_sub + conv_kernel[offset][None, None, :] * grad_pad[:, start : start + frames]
        kernel_rows.append(jnp.sum(grad_f * sub_pad[:, offset : offset + frames], axis=(0, 1)))
    kernel_local = jnp.stack(kernel_rows)
    d_sub_bf = d_sub.astype(jnp.bfloat16)
    w_out_term = jnp.einsum("rid,rie->de", attended, d_sub_bf, preferred_element_type=jnp.float32)
    d_att = jnp.einsum("rie,de->rid", d_sub_bf, w_out, preferred_element_type=jnp.float32).astype(
        jnp.bfloat16
    )
    d_att_heads = split_heads(d_att)
    row_delta = jnp.sum(
        d_att_heads.astype(jnp.float32) * split_heads(attended).astype(jnp.float32), axis=-1
    )
    row_delta = jnp.transpose(row_delta, (0, 2, 1))
    d_probs = jnp.einsum("rihe,rjhe->rhij", d_att_heads, v_all, preferred_element_type=jnp.float32)
    d_scores = (attn_probs.astype(jnp.float32) * (d_probs - row_delta[..., None])).astype(
        jnp.bfloat16
    )
    d_query = (
        jnp.einsum("rhij,rjhe->rihe", d_scores, k_all, preferred_element_type=jnp.float32)
        * inv_root
    )
    d_query = d_query.reshape(n_recs, frames, model_width).astype(jnp.bfloat16)
    d_key_term = (
        jnp.einsum("rhij,rihe->rjhe", d_scores, q_heads, preferred_element_type=jnp.float32)
        * inv_root
    )
    d_val_term = jnp.einsum(
        "rhij,rihe->rjhe", attn_probs, d_att_heads, preferred_element_type=jnp.float32
    )
    key_terms = jnp.concatenate(
        [
            d_key_term.reshape(n_recs, all_frames, model_width),
            d_val_term.reshape(n_recs, all_frames, model_width),
        ],
        axis=2,
    )
    summed = lax.psum_scatter(key_terms, "ctx", scatter_dimension=1, tiled=True)
    d_key = summed[:, :, :model_width].astype(jnp.bfloat16)
    d_value = summed[:, :, model_width:].astype(jnp.bfloat16)
    qkv_grads = jnp.concatenate([d_query, d_key, d_value], axis=2)
    d_input = jnp.einsum(
        "rif,df->rid", qkv_grads, w_qkv, preferred_element_type=jnp.float32
    ).astype(jnp.bfloat16)
    qkv_term = jnp.einsum("rid,rif->df", layer_in, qkv_grads, preferred_element_type=jnp.float32)
    d_w_qkv, d_w_out = (
        lax.psum_scatter(qkv_term, ("ctx", "rec"), scatter_dimension=0, tiled=True),
        lax.psum_scatter(w_out_term, ("ctx", "rec"), scatter_dimension=0, tiled=True),
    )
    d_kernel = lax.psum(kernel_local, ("ctx", "rec"))
    return (d_input, d_w_qkv, d_w_out, d_kernel)


def solution(mesh):
    in_specs = (
        P("rec", "ctx", None),
        P("rec", "ctx", None),
        P("rec", "ctx", None),
        P("rec", "ctx", None),
        P("rec"),
        P(),
        P(),
        P(),
        P("rec", "ctx", None),
    )
    out_specs = (P("rec", "ctx", None), P(("ctx", "rec"), None), P(("ctx", "rec"), None), P())
    return jax.shard_map(shards, mesh=mesh, in_specs=in_specs, out_specs=out_specs, check_vma=False)
```

profile of v0, /device:TPU:1, one launch (start us, length us, event | category | flops | bytes accessed | tf_op | source)
XLA Modules:
  0.0 1661.4 jit_solution(4488994573859670587)
XLA Ops:
  7.2 0.0 copy-start
  7.2 0.0 all-gather.3.cloned.1.call-start
  7.2 2.2 copy.32
  9.4 0.0 all-gather.3.cloned.1.call-update
  9.4 0.0 all-gather.5.cloned.1.call-start
  9.5 0.7 all-gather.5.cloned.1.call-update
  10.2 0.0 reduce-scatter.6.cloned.1.call-start
  10.9 1.2 copy.46
  12.1 0.0 copy-start.6
  12.2 59.5 %all-gather.3.cloned.1.call-done = bf16[1,2048,1024]{1,2,0:T(8,128)(2,1)} async-done(((bf16[1,256,1024]{1,2,0:T(8,128)(2,1)}), bf16[1,2048,1024]{1,2,0:T(8,128)(2,1)}) %all-gather.3.cloned.1.call-update) | async-done | bytes 4194320 | tf_op jit(solution)/shard_map/all_gather | solution.py:35
  71.7 4.6 fusion
  76.3 0.0 copy-done.6
  76.3 3.8 exponential_reduce_fusion
  80.0 5.2 exponential_convert_fusion
  85.2 43.6 %all-gather.5.cloned.1.call-done = bf16[1,2048,1024]{2,1,0:T(8,128)(2,1)} async-done(((bf16[1,256,1024]{2,1,0:T(8,128)(2,1)}), bf16[1,2048,1024]{2,1,0:T(8,128)(2,1)}) %all-gather.5.cloned.1.call-update) | async-done | bytes 4194320 | tf_op jit(solution)/shard_map/all_gather | solution.py:36
  128.8 6.5 copy.35
  135.3 7.6 convolution_convert_fusion.3
  142.9 0.0 copy-start.4
  142.9 0.0 copy-done
  142.9 0.7 fusion.2
  143.6 0.0 copy-done.3
  143.7 1.3 collective-permute-start
  145.0 1.5 collective-permute-start.1
  146.5 0.0 collective-permute-done
  146.5 2.9 collective-permute-done.1
  149.5 0.0 copy-done.4
  149.5 0.3 pad_maximum_fusion.1
  149.8 0.2 fusion.22
  149.9 1.2 fusion.12
  151.1 0.8 copy-done.9
  151.9 1.5 convolution_convert_fusion.1
  153.4 1.2 copy.47
  154.7 1.2 copy.38
  155.9 0.0 slice-start
  155.9 1.3 multiply_reduce_fusion
  157.3 0.0 slice-start.1
  157.3 8.1 fusion.31
  165.4 0.0 slice-done.1
  165.4 7.1 multiply_convert_fusion
  172.5 5.2 convolution_multiply_fusion
  177.7 0.6 copy-done.2
  178.3 6.2 pad_maximum_fusion
  184.5 0.0 reduce-scatter.6.cloned.1.call-update
  184.5 0.0 reduce-scatter.8.cloned.1.call-start
  184.6 1.0 copy-done.5
  185.6 0.2 copy-done.10
  185.7 2.7 fusion.25
  188.4 0.0 reduce-scatter.8.cloned.1.call-update
  188.4 0.0 copy-start.11
  188.4 0.3 reduce-scatter.10.cloned.1.call-start
  188.7 7.5 fusion.1
  196.2 165.2 %reduce-scatter.6.cloned.1.call-done = f32[1,256,2048]{1,2,0:T(8,128)} async-done(((f32[1,2048,2048]{1,2,0:T(8,128)}), f32[1,256,2048]{1,2,0:T(8,128)}) %reduce-scatter.6.cloned.1.call-update) | async-done | bytes 2097168 | tf_op jit(solution)/shard_map/reduce_scatter | solution.py:99
  361.4 1.7 convert.7
  363.1 6.3 convolution_bitcast_fusion
  369.4 0.0 copy-done.8
  369.4 12.6 copy.44
  382.0 0.0 reduce-scatter.10.cloned.1.call-update
  382.0 0.0 copy-start.1
  382.0 2.4 fusion.21
  384.4 0.1 stack.51
  384.5 65.2 %psum.7 = f32[9,1024]{1,0:T(8,128)} all-reduce(f32[9,1024]{1,0:T(8,128)S(1)} %stack.51), channel_id=1, replica_groups=mesh['ctx'=8,'rec'=16] {'ctx','rec'}, use_global_device_ids=true, to_apply=%region_15.16 | all-reduce | flops 9216 | bytes 73728 | tf_op jit(solution)/shard_map/psum | solution.py:111
  449.7 5.9 fusion.3
  455.6 544.9 %reduce-scatter.8.cloned.1.call-done = f32[8,1024]{1,0:T(8,128)} async-done(((f32[1024,1024]{1,0:T(8,128)}), f32[8,1024]{1,0:T(8,128)}) %reduce-scatter.8.cloned.1.call-update) | async-done | bytes 32784 | tf_op jit(solution)/shard_map/reduce_scatter | solution.py:109
  1000.5 654.4 %reduce-scatter.10.cloned.1.call-done = f32[8,3072]{1,0:T(8,128)} async-done(((f32[1024,3072]{1,0:T(8,128)}), f32[8,3072]{1,0:T(8,128)}) %reduce-scatter.10.cloned.1.call-update) | async-done | bytes 98320
  (20 shorter events, 0.1 us)
Async XLA Ops:
  7.2 135.7 %copy-start = (bf16[1024,1024]{1,0:T(8,128)(2,1)S(1)}, bf16[1024,1024]{1,0:T(8,128)(2,1)}, u32[]{:S(2)}) copy-start(bf16[1024,1024]{1,0:T(8,128)(2,1)} %param.15) | copy-start | bytes 6291460
  7.2 64.5 %all-gather.3.cloned.1.call-start = ((), (), s32[]{:S(2)}) async-start(), calls=%async_computation.3 | async-start | bytes 4718592 | tf_op jit(solution)/shard_map/all_gather | solution.py:35
  9.4 119.4 %all-gather.5.cloned.1.call-start = ((), (), s32[]{:S(2)}) async-start(), calls=%async_computation.4 | async-start | bytes 4718592 | tf_op jit(solution)/shard_map/all_gather | solution.py:36
  10.2 351.2 %reduce-scatter.6.cloned.1.call-start = ((), (), s32[]{:S(2)}) async-start(), calls=%async_computation.5 | async-start | bytes 18874368 | tf_op jit(solution)/shard_map/reduce_scatter | solution.py:99
  12.1 64.1 %copy-start.6 = (bf16[1,256,1024]{1,2,0:T(8,128)(2,1)}, bf16[1,256,1024]{1,2,0:T(8,128)(2,1)S(1)}, u32[]{:S(2)}) copy-start(bf16[1,256,1024]{1,2,0:T(8,128)(2,1)S(1)} %copy.46) | copy-start | bytes 1572868
  135.3 8.3 copy-start.3
  135.3 11.1 copy-start.13
  142.9 6.6 copy-start.4
  143.7 2.8 collective-permute-start
  145.0 4.5 collective-permute-start.1
  151.1 0.8 copy-start.9
  155.9 9.4 slice-start
  157.3 8.1 slice-start.1
  165.4 7.1 copy-start.7
  172.5 5.8 copy-start.2
  184.5 1.0 copy-start.5
  184.5 1.2 copy-start.10
  184.5 816.0 %reduce-scatter.8.cloned.1.call-start = ((), (), s32[]{:S(2)}) async-start(), calls=%async_computation.6 | async-start | bytes 4227072 | tf_op jit(solution)/shard_map/reduce_scatter | solution.py:109
  188.4 174.7 %copy-start.11 = (bf16[1,256,1024]{2,1,0:T(8,128)(2,1)S(1)}, bf16[1,256,1024]{2,1,0:T(8,128)(2,1)}, u32[]{:S(2)}) copy-start(bf16[1,256,1024]{2,1,0:T(8,128)(2,1)} %param.9) | copy-start | bytes 1572868
  188.4 1466.5 %reduce-scatter.10.cloned.1.call-start = ((), (), s32[]{:S(2)}) async-start(), calls=%async_computation.7 | async-start | bytes 12681216
  196.2 173.2 %copy-start.12 = (bf16[8,256,128]{1,2,0:T(8,128)(2,1)}, bf16[8,256,128]{1,2,0:T(8,128)(2,1)S(1)}, u32[]{:S(2)}) copy-start(bf16[8,256,128]{1,2,0:T(8,128)(2,1)S(1)} %fusion.1) | copy-start | bytes 1572868
  363.1 6.3 copy-start.8
  382.0 1272.9 %copy-start.1 = (bf16[1024,1024]{1,0:T(8,128)(2,1)S(1)}, bf16[1024,1024]{1,0:T(8,128)(2,1)}, u32[]{:S(2)}) copy-start(bf16[1024,1024]{1,0:T(8,128)(2,1)} %param.15) | copy-start | bytes 6291460
Sparse Core Ops, SparseCore 0:
  10.2 61.4 all-gather.2
  73.3 55.4 all-gather.4
  184.7 176.7 reduce-scatter.5
  364.2 636.2 reduce-scatter.7
  1003.5 651.3 reduce-scatter.9
where the time goes:
time: 1670 us; the launch traced here: 1660 us
  waiting for transfers between devices  1470 us (88%)
  blocking collectives  65.2 us (4%)
  matrix products  57.2 us (3%)
  local copies, waits for them, and re-layouts  27.7 us (2%)
  other arithmetic  22.2 us (1%)
    unnamed x6, waiting for transfers between devices  655 us
    reduce_scatter x1, waiting for transfers between devices, shards(): lax.psum_scatter(w_out_term, ('ctx', 'rec'), scatter_dimension=0, tiled=T...  545 us
    reduce_scatter x1, waiting for transfers between devices, shards(): summed = lax.psum_scatter(key_terms, 'ctx', scatter_dimension=1, tiled=True)  165 us
    psum x1, blocking collectives, shards(): d_kernel = lax.psum(kernel_local, ('ctx', 'rec'))  65.2 us
    all_gather x1, waiting for transfers between devices, shards(): lax.all_gather(keys, 'ctx', axis=1, tiled=True)  59.5 us
    all_gather x1, waiting for transfers between devices, shards(): lax.all_gather(values, 'ctx', axis=1, tiled=True)  43.6 us
  transfers between devices with their start and end apart: 7, of which 6 were waited for; matrix products, arithmetic and copies ran while one was open for 3% of the time, Pallas kernels for 0%

commit v1 on v0

v1 whole, which is shorter than its diff:
```python
import math

import jax
import jax.numpy as jnp
from jax import lax
from jax.experimental import pallas as pl
from jax.experimental.pallas import tpu as pltpu
from jax.sharding import PartitionSpec as P

HD = 128
KW = 9
NC = 8
BF = 256
T = NC * BF
D = 1024
F32 = jnp.float32
BF16 = jnp.bfloat16
MESH = pl.DeviceIdType.MESH
KB = 512
NEG = -1e30
NT = (((1,), (1,)), ((), ()))
ANY = pl.BlockSpec(memory_space=pl.ANY)
VM = pl.BlockSpec(memory_space=pltpu.VMEM)

TQ, TK, TV, TD, BA, BQ, BK, BV = range(8)


def mult(value, of):
    return pl.multiple_of(value, of)


def dot(a, b):
    return jnp.dot(a, b, preferred_element_type=F32)


def dot_nt(a, b):
    return lax.dot_general(a, b, NT, preferred_element_type=F32)


def attention_kernel(
    len_ref, q_ref, k_ref, v_ref, g_ref, conv_ref, wout_ref,
    att_out, dsub_out, dqkv_out, dker_out,
    q_aug, k_aug, v_aug, do_in, do_aug, k_t, v_t, s_ref, e_ref, ds_ref,
    att_s, linv_s, dq_s, dk_s, dv_s, dat_s, att_fr, dq_fr, dk_fr, dv_fr,
    g_vm, gp, halo_lo, halo_hi, wout_vm,
    send_sem, recv_sem, halo_send, halo_recv, local_sem,
):
    me = lax.axis_index("ctx")
    rec = lax.axis_index("rec")
    z, y = lax.div(me, 4), lax.rem(me, 4)
    inv_root = 1.0 / math.sqrt(HD)
    c_exp = math.log2(math.e) / math.sqrt(HD)

    def peer(d):
        return lax.rem(z + lax.div(d, 4), 2) * 4 + lax.rem(y + lax.rem(d, 4), 4)

    def origin(d):
        return lax.rem(z + 2 - lax.div(d, 4), 2) * 4 + lax.rem(y + 4 - lax.rem(d, 4), 4)

    def head_cols(h):
        return pl.ds(mult(h * HD, HD), HD)

    def slot(d):
        return pl.ds(mult(d * BF, BF), BF)

    fwd_src = {TQ: q_ref, TK: k_ref, TV: v_ref}
    fwd_dst = {TQ: q_aug, TK: k_aug, TV: v_aug, TD: do_in}
    back_src = {BA: att_s, BQ: dq_s, BK: dk_s, BV: dv_s}
    back_dst = {BA: att_fr, BQ: dq_fr, BK: dk_fr, BV: dv_fr}

    def ends(t, d):
        if t <= TD:
            p = peer(d)
            src = dat_s.at[d] if t == TD else fwd_src[t].at[:, head_cols(p)]
            dst = fwd_dst[t].at[slot(d), pl.ds(0, HD)]
        else:
            p = origin(d)
            src = back_src[t].at[d]
            dst = back_dst[t].at[:, head_cols(me)]
        return p, src, dst

    def remote(t, d):
        p, src, dst = ends(t, d)
        return pltpu.make_async_remote_copy(
            src_ref=src, dst_ref=dst, send_sem=send_sem.at[t, d], recv_sem=recv_sem.at[t, d],
            device_id=(p, rec), device_id_type=MESH,
        )

    def local(t):
        _, src, dst = ends(t, 0)
        return pltpu.make_async_copy(src, dst, recv_sem.at[t, 0])

    def each_peer(body):
        def step(d, carry):
            body(d)
            return carry

        lax.fori_loop(1, NC, step, 0)

    def each_slot(body):
        def step(d, carry):
            body(d)
            return carry

        lax.fori_loop(0, NC, step, 0)

    get_g = pltpu.make_async_copy(g_ref, g_vm, local_sem.at[0])
    get_w = pltpu.make_async_copy(wout_ref, wout_vm, local_sem.at[1])
    get_g.start()
    get_w.start()
    for t in (TK, TQ, TV):
        local(t).start()

    barrier = pltpu.get_barrier_semaphore()
    each_peer(
        lambda d: pl.semaphore_signal(barrier, inc=1, device_id=(peer(d), rec), device_id_type=MESH)
    )
    pl.semaphore_wait(barrier, NC - 1)

    right, left = lax.rem(me + 1, NC), lax.rem(me + NC - 1, NC)
    to_right = pltpu.make_async_remote_copy(
        src_ref=g_ref.at[pl.ds(BF - 16, 16), :], dst_ref=halo_lo, send_sem=halo_send.at[0],
        recv_sem=halo_recv.at[0], device_id=(right, rec), device_id_type=MESH,
    )
    to_left = pltpu.make_async_remote_copy(
        src_ref=g_ref.at[pl.ds(0, 16), :], dst_ref=halo_hi, send_sem=halo_send.at[1],
        recv_sem=halo_recv.at[1], device_id=(left, rec), device_id_type=MESH,
    )
    to_right.start()
    to_left.start()
    for t in (TK, TQ, TV):
        each_peer(lambda d: remote(t, d).start())

    length = len_ref[0]
    lane = lax.broadcasted_iota(jnp.int32, (BF, HD), 1)
    row = lax.broadcasted_iota(jnp.int32, (BF, HD), 0)

    def extra(d):
        masked = (lane == 0) & (row + origin(d) * BF >= length)
        k_aug[slot(d), pl.ds(HD, HD)] = jnp.where(masked, NEG, 0.0).astype(BF16)
        q_aug[slot(d), pl.ds(HD, HD)] = jnp.where(lane == 0, 1.0, 0.0).astype(BF16)
        v_aug[slot(d), pl.ds(HD, HD)] = jnp.where(lane < 2, 1.0, 0.0).astype(BF16)

    each_slot(extra)
    first = lax.broadcasted_iota(jnp.int32, (16, T), 0) == 0
    v_t[pl.ds(HD, 16), :] = jnp.where(first, 1.0, 0.0).astype(BF16)

    get_g.wait()
    gp[pl.ds(8, BF), :] = g_vm[...].astype(F32)
    to_right.wait_recv()
    to_left.wait_recv()
    low = halo_lo[...].astype(F32)[8:16, :]
    gp[pl.ds(0, 8), :] = jnp.where(me > 0, low, 0.0)
    high = halo_hi[...].astype(F32)[0:8, :]
    gp[pl.ds(8 + BF, 8), :] = jnp.where(me < NC - 1, high, 0.0)

    def conv_grad(n):
        cols = pl.ds(mult(n * HD, HD), HD)
        total = gp[pl.ds(8, BF), cols]
        for t in range(KW):
            total = total + conv_ref[pl.ds(t, 1), cols] * gp[pl.ds(12 - t, BF), cols]
        dsub_out[:, cols] = total.astype(BF16)

    each_slot(conv_grad)

    get_w.wait()

    def datt(d):
        rows = pl.ds(mult(peer(d) * HD, HD), HD)
        dat_s[d] = dot_nt(dsub_out[...], wout_vm[rows, :]).astype(BF16)

        @pl.when(d > 0)
        def _():
            remote(TD, d).start()

    each_slot(datt)
    local(TD).start()

    for t in (TK, TV):
        local(t).wait()
        each_peer(lambda d: remote(t, d).wait_recv())

    def turn(d):
        k_t[:, slot(d)] = k_aug[slot(d), pl.ds(0, HD)].T
        v_t[pl.ds(0, HD), slot(d)] = v_aug[slot(d), pl.ds(0, HD)].T

    each_slot(turn)
    local(TQ).wait()

    def forward(d):
        @pl.when(d > 0)
        def _():
            remote(TQ, d).wait_recv()

        qd = q_aug[slot(d), :]
        top = None
        for b in range(T // KB):
            rows = pl.ds(b * KB, KB)
            s = dot_nt(k_aug[rows, :], qd)
            s_ref[rows, :] = s
            m = jnp.max(s, axis=0, keepdims=True)
            top = m if top is None else jnp.maximum(top, m)
        acc = jnp.zeros((HD + 16, BF), F32)
        for b in range(T // KB):
            rows = pl.ds(b * KB, KB)
            e = jnp.exp2((s_ref[rows, :] - top) * c_exp).astype(BF16)
            e_ref[rows, slot(d)] = e
            acc = acc + dot(v_t[:, rows], e)
        inv = 1.0 / acc[HD : HD + 1, :]
        att_s[d] = (acc[:HD, :] * inv).T.astype(BF16)
        linv_s[d] = jnp.broadcast_to(inv, (HD, BF)).T

        @pl.when(d > 0)
        def _():
            remote(BA, d).start()

    each_slot(forward)
    local(BA).start()

    local(TD).wait()

    def backward_in(d):
        @pl.when(d > 0)
        def _():
            remote(TD, d).wait_recv()

        do = (do_in[slot(d), :].astype(F32) * linv_s[d]).astype(BF16)
        delta = -jnp.sum(do.astype(F32) * att_s[d].astype(F32), axis=1, keepdims=True)
        hi = delta.astype(BF16).astype(F32)
        do_aug[slot(d), pl.ds(0, HD)] = do
        do_aug[slot(d), pl.ds(HD, HD)] = jnp.where(
            lane == 0, hi, jnp.where(lane == 1, delta - hi, 0.0)
        ).astype(BF16)

    each_slot(backward_in)

    def d_value(j):
        dv_s[j] = dot(e_ref[slot(j), :], do_aug[:, pl.ds(0, HD)]).astype(BF16)

        @pl.when(j > 0)
        def _():
            remote(BV, j).start()

    each_slot(d_value)
    local(BV).start()

    def d_query(d):
        dod = do_aug[slot(d), :]
        acc = jnp.zeros((HD, BF), F32)
        for b in range(T // KB):
            rows = pl.ds(b * KB, KB)
            dp = dot_nt(v_aug[rows, :], dod)
            ds = (e_ref[rows, slot(d)].astype(F32) * dp).astype(BF16)
            ds_ref[rows, slot(d)] = ds
            acc = acc + dot(k_t[:, rows], ds)
        dq_s[d] = (acc * inv_root).T.astype(BF16)

        @pl.when(d > 0)
        def _():
            remote(BQ, d).start()

    each_slot(d_query)
    local(BQ).start()

    def d_key(j):
        dk = dot(ds_ref[slot(j), :], q_aug[:, pl.ds(0, HD)])
        dk_s[j] = (dk * inv_root).astype(BF16)

        @pl.when(j > 0)
        def _():
            remote(BK, j).start()

    each_slot(d_key)
    local(BK).start()

    local(BA).wait()
    each_peer(lambda d: remote(BA, d).wait_recv())
    att_out[...] = att_fr[...]

    def taps(n):
        cols = pl.ds(mult(n * BF, BF), BF)
        sub = dot(att_fr[...], wout_vm[:, cols]).astype(BF16).astype(F32)
        for t in range(KW):
            dker_out[pl.ds(t, 1), cols] = jnp.sum(
                sub * gp[pl.ds(12 - t, BF), cols], axis=0, keepdims=True
            )

    dker_out[...] = jnp.zeros_like(dker_out)
    lax.fori_loop(0, D // BF, lambda n, c: (taps(n), c)[1], 0)

    for part, (t, ref) in enumerate(((BQ, dq_fr), (BK, dk_fr), (BV, dv_fr))):
        local(t).wait()
        each_peer(lambda d: remote(t, d).wait_recv())
        dqkv_out[:, pl.ds(part * D, D)] = ref[...]

    to_right.wait_send()
    to_left.wait_send()
    for t in range(8):
        each_peer(lambda d: remote(t, d).wait_send())


def attention(lengths, q, k, v, g, conv, wout):
    def vm(shape, dtype=BF16):
        return pltpu.VMEM(shape, dtype)

    return pl.pallas_call(
        attention_kernel,
        out_shape=(
            jax.ShapeDtypeStruct((BF, D), BF16),
            jax.ShapeDtypeStruct((BF, D), BF16),
            jax.ShapeDtypeStruct((BF, 3 * D), BF16),
            jax.ShapeDtypeStruct((16, D), F32),
        ),
        in_specs=[pl.BlockSpec(memory_space=pltpu.SMEM), ANY, ANY, ANY, ANY, VM, ANY],
        out_specs=(VM, VM, VM, VM),
        scratch_shapes=[
            vm((T, 2 * HD)), vm((T, 2 * HD)), vm((T, 2 * HD)), vm((T, HD)), vm((T, 2 * HD)),
            vm((HD, T)), vm((HD + 16, T)), vm((T, BF), F32), vm((T, T)), vm((T, T)),
            vm((NC, BF, HD)), vm((NC, BF, HD), F32), vm((NC, BF, HD)), vm((NC, BF, HD)),
            vm((NC, BF, HD)), vm((NC, BF, HD)), vm((BF, D)), vm((BF, D)), vm((BF, D)), vm((BF, D)),
            vm((BF, D)), vm((BF + 16, D), F32), vm((16, D)), vm((16, D)), vm((D, D)),
            pltpu.SemaphoreType.DMA((8, NC)), pltpu.SemaphoreType.DMA((8, NC)),
            pltpu.SemaphoreType.DMA((2,)), pltpu.SemaphoreType.DMA((2,)), pltpu.SemaphoreType.DMA((2,)),
        ],
        compiler_params=pltpu.CompilerParams(
            collective_id=0, has_side_effects=True, vmem_limit_bytes=56 * 1024 * 1024
        ),
    )(lengths, q, k, v, g, conv, wout)


HALF = 512
CW = 4 * HALF
PARTS = (
    (0, 384, 768, ("x", "y", "z")),
    (768, 384, 640, ("y", "z", "x")),
    (1408, 384, 640, ("z", "x", "y")),
)
LEFT = {"x": 0, "y": 1, "z": 2}


def weights_kernel(
    li_ref, dqkv_ref, att_ref, dsub_ref, dker_ref, wqkv_ref,
    din_out, dwq_out, dwo_out, dk_out,
    li2, att2, r2, li_t, att_t, grads, fin, fin_x, taps_c, taps_a, *rest,
):
    bufs = rest[:36]
    core_send, core_recv, ring_send, ring_recv, taps_send, taps_recv = rest[36:]
    ctx = lax.axis_index("ctx")
    rec = lax.axis_index("rec")
    core = lax.rem(rec, 2)
    other = 1 - core
    at = {
        "x": lax.rem(lax.div(rec, 2), 4),
        "y": lax.rem(ctx, 4),
        "z": lax.div(rec, 8) * 2 + lax.div(ctx, 4),
    }

    def device(moved, to, on_core=core):
        p = {**at, **({moved: to} if moved else {})}
        return (
            lax.rem(p["z"], 2) * 4 + p["y"],
            lax.div(p["z"], 2) * 8 + p["x"] * 2 + on_core,
        )

    def off(axis, by):
        return lax.rem(at[axis] + by, 4)

    partner = device(None, None, other)

    barrier = pltpu.get_barrier_semaphore()
    greet = [partner] + [device(a, off(a, by)) for a in "xyz" for by in (1, 2, 3)]
    for who in greet:
        pl.semaphore_signal(barrier, inc=1, device_id=who, device_id_type=MESH)
    pl.semaphore_wait(barrier, len(greet))

    def to_partner(n, src, dst):
        return pltpu.make_async_remote_copy(
            src_ref=src, dst_ref=dst, send_sem=core_send.at[n], recv_sem=core_recv.at[n],
            device_id=partner, device_id_type=MESH,
        )

    def half(ref, base, c):
        return ref.at[:, pl.ds(mult(base + c * HALF, HALF), HALF)]

    theirs = pl.ds(BF, BF)
    swaps = [
        to_partner(0, li_ref, li2.at[theirs, :]),
        to_partner(1, half(dqkv_ref, 0, other), r2.at[theirs, pl.ds(0, HALF)]),
        to_partner(2, half(dqkv_ref, D, other), r2.at[theirs, pl.ds(HALF, HALF)]),
        to_partner(3, half(dqkv_ref, 2 * D, other), r2.at[theirs, pl.ds(2 * HALF, HALF)]),
        to_partner(4, att_ref, att2.at[theirs, :]),
        to_partner(5, half(dsub_ref, 0, other), r2.at[theirs, pl.ds(3 * HALF, HALF)]),
        to_partner(6, dker_ref, taps_c.at[core]),
    ]
    for swap in swaps:
        swap.start()
    mine = pl.ds(0, BF)
    li2[mine, :] = li_ref[...]
    att2[mine, :] = att_ref[...]
    for n in range(3):
        r2[mine, pl.ds(n * HALF, HALF)] = dqkv_ref[:, pl.ds(mult(n * D + core * HALF, HALF), HALF)]
    r2[mine, pl.ds(3 * HALF, HALF)] = dsub_ref[:, pl.ds(mult(core * HALF, HALF), HALF)]
    taps_c[core] = dker_ref[...]
    for swap in swaps:
        swap.wait_recv()

    def turn(n, carry):
        cols = pl.ds(mult(n * BF, BF), BF)
        li_t[cols, :] = li2[:, cols].T
        att_t[cols, :] = att2[:, cols].T
        return carry

    lax.fori_loop(0, 4, turn, 0)

    def product(lhs, start, width):
        def step(b, carry):
            rows = pl.ds(mult(b * HD, HD), HD)
            g = dot(lhs[rows, :], r2[:, pl.ds(start, width)]).astype(BF16)
            grads[lax.div(b, 4), lax.rem(b, 4), :, :, :, pl.ds(start, width)] = g.reshape(
                2, 4, 16, width
            )
            return carry

        lax.fori_loop(0, 8, step, 0)

    def region(fixed, start, width):
        zl = zh = slice(None)
        if "z" in fixed:
            zl, zh = lax.rem(fixed["z"], 2), lax.div(fixed["z"], 2)
        return grads.at[
            zl, fixed.get("y", slice(None)), zh, fixed.get("x", slice(None)), :, pl.ds(start, width)
        ]

    class Ring:
        def __init__(self, part, stage):
            self.start, self.wide_a, self.width, order = PARTS[part]
            self.wide_b = self.width - self.wide_a
            self.axis = order[stage]
            self.fixed = {a: at[a] for a in order[:stage]}
            base = (part * 3 + stage) * 4
            self.ra, self.rb, self.low, self.high = bufs[base : base + 4]
            self.sems = (part * 3 + stage) * 6
            self.stage = stage
            a = self.wide_a
            lead = len(self.low.shape) - 1

            def cols(ref, half_b):
                pick = pl.ds(a, self.wide_b) if half_b else pl.ds(0, a)
                return ref.at[(slice(None),) * lead + (pick,)]

            self.cols = cols
            low, high = self.low, self.high
            self.copies = [
                self.copy(0, self.piece(2, 0), self.ra, 1),
                self.copy(1, self.piece(2, 1), self.rb, 3),
                self.copy(2, self.piece(1, 1), cols(low, 1), 1),
                self.copy(3, self.piece(3, 0), cols(high, 0), 3),
                self.copy(4, self.piece(1, 0), cols(low, 0), 1),
                self.copy(5, self.piece(3, 1), cols(high, 1), 3),
            ]

        def piece(self, by, half_b=None):
            start, width = self.start, self.width
            if half_b is not None:
                start, width = (
                    (start + self.wide_a, self.wide_b) if half_b else (start, self.wide_a)
                )
            return region({**self.fixed, self.axis: off(self.axis, by)}, start, width)

        def copy(self, n, src, dst, by):
            return pltpu.make_async_remote_copy(
                src_ref=src, dst_ref=dst, send_sem=ring_send.at[self.sems + n],
                recv_sem=ring_recv.at[self.sems + n],
                device_id=device(self.axis, off(self.axis, by)), device_id_type=MESH,
            )

        def begin(self):
            for c in self.copies[:4]:
                c.start()

        def relay(self):
            for n, by, buf, half_b in ((0, 1, self.ra, 0), (1, 3, self.rb, 1)):
                self.copies[n].wait_recv()
                here = self.piece(by, half_b)
                here[...] = (here[...].astype(F32) + buf[...].astype(F32)).astype(BF16)
                self.copies[4 + n].start()

        def end(self):
            for n in (2, 3, 4, 5):
                self.copies[n].wait_recv()
            here = self.piece(0)
            total = here[...].astype(F32) + self.low[...].astype(F32) + self.high[...].astype(F32)
            if self.stage < 2:
                here[...] = total.astype(BF16)
            else:
                fin[:, pl.ds(self.start, self.width)] = total

        def sent(self):
            for c in self.copies:
                c.wait_send()

    rings = [[Ring(p, s) for s in range(3)] for p in range(3)]

    product(li_t, 0, 768)
    rings[0][0].begin()
    product(li_t, 768, 640)
    rings[1][0].begin()
    product(li_t, 1408, 128)
    product(att_t, 1536, 512)
    rings[2][0].begin()

    taps_copies = []

    def taps_send_on(n, axis, value):
        taps_a[n, at[axis]] = value
        for by in (1, 2, 3):
            c = pltpu.make_async_remote_copy(
                src_ref=taps_a.at[n, at[axis]], dst_ref=taps_a.at[n, at[axis]],
                send_sem=taps_send.at[n * 3 + by - 1], recv_sem=taps_recv.at[n * 3 + by - 1],
                device_id=device(axis, off(axis, by)), device_id_type=MESH,
            )
            c.start()
            taps_copies.append(c)

    def taps_sum(n):
        for c in taps_copies[n * 3 :]:
            c.wait_recv()
        return (taps_a[n, 0] + taps_a[n, 1]) + (taps_a[n, 2] + taps_a[n, 3])

    taps_send_on(0, "x", taps_c[0] + taps_c[1])

    def d_input(n, carry):
        cols = pl.ds(mult(n * BF, BF), BF)
        din_out[:, cols] = dot_nt(dqkv_ref[...], wqkv_ref[cols, :]).astype(BF16)
        return carry

    lax.fori_loop(0, 2, d_input, 0)
    for r in rings:
        r[0].relay()
    taps_send_on(1, "y", taps_sum(0))
    lax.fori_loop(2, 4, d_input, 0)
    for stage in (0, 1):
        for r in rings:
            r[stage].end()
            r[stage + 1].begin()
        if stage == 0:
            taps_send_on(2, "z", taps_sum(1))
        for r in rings:
            r[stage + 1].relay()
    dk_out[...] = taps_sum(2)
    for r in rings:
        r[2].end()

    last = to_partner(7, fin.at[pl.ds(mult(other * 8, 8), 8), :], fin_x)
    last.start()
    for who, ref in ((core, fin), (other, fin_x)):
        if ref is fin_x:
            last.wait_recv()
            block = fin_x[...]
        else:
            block = fin[pl.ds(mult(core * 8, 8), 8), :]
        for n in range(3):
            dwq_out[:, pl.ds(mult(n * D + who * HALF, HALF), HALF)] = block[
                :, n * HALF : (n + 1) * HALF
            ]
        dwo_out[:, pl.ds(mult(who * HALF, HALF), HALF)] = block[:, 3 * HALF :]

    last.wait_send()
    for swap in swaps:
        swap.wait_send()
    for c in taps_copies:
        c.wait_send()
    for r in rings:
        for ring in r:
            ring.sent()


def weights(layer_in, dqkv, att, dsub, dker, wqkv):
    def vm(shape, dtype=BF16):
        return pltpu.VMEM(shape, dtype)

    buffers = []
    for start, wide_a, width, order in PARTS:
        for stage in range(3):
            lead = []
            for axis, sizes in (("zl", 2), ("y", 4), ("zh", 2), ("x", 4)):
                if axis[0] not in order[: stage + 1]:
                    lead.append(sizes)
            for w in (wide_a, width - wide_a, width, width):
                buffers.append(vm((*lead, 16, w)))
    dma = pltpu.SemaphoreType.DMA
    return pl.pallas_call(
        weights_kernel,
        out_shape=(
            jax.ShapeDtypeStruct((BF, D), BF16),
            jax.ShapeDtypeStruct((8, 3 * D), F32),
            jax.ShapeDtypeStruct((8, D), F32),
            jax.ShapeDtypeStruct((16, D), F32),
        ),
        in_specs=[VM] * 6,
        out_specs=(VM,) * 4,
        scratch_shapes=[
            vm((2 * BF, D)), vm((2 * BF, D)), vm((2 * BF, CW)), vm((D, 2 * BF)), vm((D, 2 * BF)),
            vm((2, 4, 2, 4, 16, CW)), vm((16, CW), F32), vm((8, CW), F32),
            vm((2, 16, D), F32), vm((3, 4, 16, D), F32), *buffers,
            dma((8,)), dma((8,)), dma((54,)), dma((54,)), dma((9,)), dma((9,)),
        ],
        compiler_params=pltpu.CompilerParams(
            collective_id=1, has_side_effects=True, vmem_limit_bytes=56 * 1024 * 1024
        ),
    )(layer_in, dqkv, att, dsub, dker, wqkv)


def shards(layer_in, queries, keys, values, lengths, w_qkv, w_out, conv_kernel, grad_out):
    att, dsub, dqkv, dker = attention(
        lengths, queries[0], keys[0], values[0], grad_out[0], conv_kernel, w_out
    )
    d_input, d_wqkv, d_wout, d_kernel = weights(layer_in[0], dqkv, att, dsub, dker, w_qkv)
    return d_input[None], d_wqkv, d_wout, d_kernel[:KW]


def solution(mesh):
    frames = P("rec", "ctx", None)
    in_specs = (frames, frames, frames, frames, P("rec"), P(), P(), P(), frames)
    out_specs = (frames, P(("ctx", "rec"), None), P(("ctx", "rec"), None), P())
    return jax.shard_map(
        shards, mesh=mesh, in_specs=in_specs, out_specs=out_specs, check_vma=False
    )
```

time: 1670 us -> 125 us (0.07)
  waiting for transfers between devices: 1470 us -> 0 us
  Pallas kernels: 0 us -> 117 us
  blocking collectives: 65.2 us -> 0 us
  matrix products: 57.2 us -> 0 us
  other arithmetic: 22.2 us -> 0 us
  local copies, waits for them, and re-layouts: 27.7 us -> 6.25 us
    reduce_scatter x2 -> x0, waiting for transfers between devices: 710 us -> none  [the longest x1 545 us: shards(): lax.psum_scatter(w_out_term, ('ctx', 'rec'), scatter_dimension=0, tiled=T...]
    unnamed x6 -> x0, waiting for transfers between devices: 655 us -> none
    pallas_call x0 -> x2, Pallas kernels: none -> 117 us  [the longest x1 63.7 us: attention(): pl.pallas_call(attention_kernel, out_shape=(jax.ShapeDtypeStruct((BF, D),...]
    all_gather x2 -> x0, waiting for transfers between devices: 103 us -> none  [the longest x1 59.5 us: shards(): lax.all_gather(keys, 'ctx', axis=1, tiled=True)]
    psum x1 -> x0, blocking collectives: 65.2 us -> none  [shards(): d_kernel = lax.psum(kernel_local, ('ctx', 'rec'))]
    dot_general x11 -> x0, matrix products: 57.2 us -> none  [the longest x1 8.11 us: shards(): jnp.einsum('rhij,rihe->rjhe', attn_probs, d_att_heads, preferred_element_...]
  transfers between devices with their start and end apart: 7 -> 0, of which waited for: 6 -> 0; matrix products, arithmetic and copies ran while one was open for 3% -> 0% of each run, Pallas kernels for 0% -> 0%
where the time goes in v1:
time: 125 us
  Pallas kernels  117 us (94%)
  local copies, waits for them, and re-layouts  6.25 us (5%)
  between operations  1.3 us (1%)
    pallas_call x1, Pallas kernels, attention(): pl.pallas_call(attention_kernel, out_shape=(jax.ShapeDtypeStruct((BF, D),...  63.7 us
    pallas_call x1, Pallas kernels, weights(): pl.pallas_call(weights_kernel, out_shape=(jax.ShapeDtypeStruct((BF, D), B...  53.3 us
    unnamed x4, local copies, waits for them, and re-layouts  6.25 us

profile of v1, /device:TPU:1, one launch (start us, length us, event | category | flops | bytes accessed | tf_op | source)
XLA Modules:
  0.0 124.6 jit_solution(11132476439971138763)
XLA Ops:
  1.3 63.7 %shard_map.120 = (bf16[256,1024]{1,0:T(8,128)(2,1)}, bf16[256,1024]{1,0:T(8,128)(2,1)}, bf16[256,3072]{1,0:T(8,128)(2,1)}, f32[16,1024]{1,0:T(8,128)}) custom-call(s32[1]{0:T(128)S(6)} %copy.17.len_ref, bf16[256,1024]{1,0:T(8,128)(2,1)} %bitcast.7, bf16[256,1024]{1,0:T(8,128)(2,1)} %bitcast.8, bf16[256,1024]{1,0:T(8,128)(2,1)} %bitcast.9, ...), custom_call_target="tpu_custom_call" | custom-call | tf_op jit(solution)/shard_map/pallas_call | solution.py:306
  65.0 53.3 %shard_map.121 = (bf16[256,1024]{1,0:T(8,128)(2,1)}, f32[8,3072]{1,0:T(8,128)}, f32[8,1024]{1,0:T(8,128)}, f32[16,1024]{1,0:T(8,128)}) custom-call(bf16[256,1024]{1,0:T(8,128)(2,1)} %bitcast.11, bf16[256,3072]{1,0:T(8,128)(2,1)} %get-tuple-element.12.dqkv_ref, bf16[256,1024]{1,0:T(8,128)(2,1)} %get-tuple-element.13.att_ref, ...), custom_call_target="tpu_custom_call" | custom-call | tf_op jit(solution)/shard_map/pallas_call | solution.py:592
  118.3 1.9 %copy.18 = bf16[1,256,1024]{2,1,0:T(8,128)(2,1)} copy(bf16[1,256,1024]{2,1,0:T(8,128)(2,1)} %bitcast.12) | data formatting | bytes 1048576
  120.2 1.5 %copy.19 = f32[8,3072]{1,0:T(8,128)} copy(f32[8,3072]{1,0:T(8,128)} %get-tuple-element.25) | data formatting | bytes 196608
  121.8 1.4 %copy.20 = f32[8,1024]{1,0:T(8,128)} copy(f32[8,1024]{1,0:T(8,128)} %get-tuple-element.26) | data formatting | bytes 65536
  123.1 1.5 %copy.21 = f32[9,1024]{1,0:T(8,128)} copy(f32[9,1024]{1,0:T(8,128)} %bitcast.13) | data formatting | bytes 73728

commit v2 on v1

v2 whole, which is shorter than its diff:
```python
import math

import jax
import jax.numpy as jnp
from jax import lax
from jax.experimental import pallas as pl
from jax.experimental.pallas import tpu as pltpu
from jax.sharding import PartitionSpec as P

HD = 128
KW = 9
NC = 8
BF = 256
T = NC * BF
D = 1024
F32 = jnp.float32
BF16 = jnp.bfloat16
MESH = pl.DeviceIdType.MESH
KB = 512
NEG = -1e30
NT = (((1,), (1,)), ((), ()))
ANY = pl.BlockSpec(memory_space=pl.ANY)
VM = pl.BlockSpec(memory_space=pltpu.VMEM)

TQ, TK, TV, TD, BA, BQ, BK, BV = range(8)


def mult(value, of):
    return pl.multiple_of(value, of)


def dot(a, b):
    return jnp.dot(a, b, preferred_element_type=F32)


def dot_nt(a, b):
    return lax.dot_general(a, b, NT, preferred_element_type=F32)


HALF = 512
CW = 4 * HALF
OUT, VAL, QUE, KEY = range(4)
PARTS = (
    (0, 512, ("x", "y", "z")),
    (512, 512, ("x", "z", "y")),
    (1024, 256, ("y", "z", "x")),
    (1280, 256, ("z", "y", "x")),
    (1536, 256, ("y", "x", "z")),
    (1792, 256, ("z", "x", "y")),
)
NP = len(PARTS)


def backward_kernel(
    len_ref, li_ref, q_ref, k_ref, v_ref, g_ref, conv_ref, wout_ref, wqkv_ref,
    din_out, dwq_out, dwo_out, dk_out,
    q_aug, k_aug, v_aug, do_in, do_aug, k_t, v_t, s_ref, e_ref, ds_ref,
    att_s, linv_s, dq_s, dk_s, dv_s, dat_s, dqkv, din_vm,
    g_vm, gp, dsub, halo_lo, halo_hi, wout_vm, wqkv_vm,
    li2, att2, r2, li_t, att_t, grads, fin, fin_x, taps_c, taps_a, *rest,
):
    bufs = rest[: NP * 6]
    (send_sem, recv_sem, halo_send, halo_recv, local_sem, core_send, core_recv,
     ring_send, ring_recv, step_send, step_recv, taps_send, taps_recv) = rest[NP * 6 :]
    me = lax.axis_index("ctx")
    rec = lax.axis_index("rec")
    z, y = lax.div(me, 4), lax.rem(me, 4)
    inv_root = 1.0 / math.sqrt(HD)
    c_exp = math.log2(math.e) / math.sqrt(HD)

    def peer(d):
        return lax.rem(z + lax.div(d, 4), 2) * 4 + lax.rem(y + lax.rem(d, 4), 4)

    def origin(d):
        return lax.rem(z + 2 - lax.div(d, 4), 2) * 4 + lax.rem(y + 4 - lax.rem(d, 4), 4)

    def head_cols(h):
        return pl.ds(mult(h * HD, HD), HD)

    def slot(d):
        return pl.ds(mult(d * BF, BF), BF)

    fwd_src = {TQ: q_ref, TK: k_ref, TV: v_ref}
    fwd_dst = {TQ: q_aug, TK: k_aug, TV: v_aug, TD: do_in}
    back_src = {BA: att_s, BQ: dq_s, BK: dk_s, BV: dv_s}
    back_base = {BQ: 0, BK: D, BV: 2 * D}

    def ends(t, d):
        if t <= TD:
            p = peer(d)
            src = dat_s.at[d] if t == TD else fwd_src[t].at[:, head_cols(p)]
            dst = fwd_dst[t].at[slot(d), pl.ds(0, HD)]
        else:
            p = origin(d)
            src = back_src[t].at[d]
            if t == BA:
                dst = att2.at[pl.ds(0, BF), head_cols(me)]
            else:
                dst = dqkv.at[:, pl.ds(mult(back_base[t] + me * HD, HD), HD)]
        return p, src, dst

    def remote(t, d):
        p, src, dst = ends(t, d)
        return pltpu.make_async_remote_copy(
            src_ref=src, dst_ref=dst, send_sem=send_sem.at[t, d], recv_sem=recv_sem.at[t, d],
            device_id=(p, rec), device_id_type=MESH,
        )

    def local(t):
        _, src, dst = ends(t, 0)
        return pltpu.make_async_copy(src, dst, recv_sem.at[t, 0])

    def each_peer(body):
        def step(d, carry):
            body(d)
            return carry

        lax.fori_loop(1, NC, step, 0)

    def each_slot(body):
        def step(d, carry):
            body(d)
            return carry

        lax.fori_loop(0, NC, step, 0)

    get_g = pltpu.make_async_copy(g_ref, g_vm, local_sem.at[0])
    get_w = pltpu.make_async_copy(wout_ref, wout_vm, local_sem.at[1])
    get_g.start()
    get_w.start()
    for t in (TK, TV, TQ):
        local(t).start()
    mine, theirs = pl.ds(0, BF), pl.ds(BF, BF)
    get_li = pltpu.make_async_copy(li_ref, li2.at[mine, :], local_sem.at[2])
    get_li.start()
    get_wq = pltpu.make_async_copy(wqkv_ref, wqkv_vm, local_sem.at[3])

    core = lax.rem(rec, 2)
    other = 1 - core
    at = {"x": lax.rem(lax.div(rec, 2), 4), "y": y, "z": lax.div(rec, 8) * 2 + z}

    def device(moved, to, on_core=core):
        p = {**at, **({moved: to} if moved else {})}
        return (
            lax.rem(p["z"], 2) * 4 + p["y"],
            lax.div(p["z"], 2) * 8 + p["x"] * 2 + on_core,
        )

    def off(axis, by):
        return lax.rem(at[axis] + by, 4)

    partner = device(None, None, other)
    far = lax.rem(lax.div(rec, 8) + 1, 2)
    greet = [partner] + [device("x", off("x", by)) for by in (1, 2, 3)]
    greet += [device("z", far * 2 + zl) for zl in (0, 1)]

    barrier = pltpu.get_barrier_semaphore()
    each_peer(
        lambda d: pl.semaphore_signal(barrier, inc=1, device_id=(peer(d), rec), device_id_type=MESH)
    )
    for who in greet:
        pl.semaphore_signal(barrier, inc=1, device_id=who, device_id_type=MESH)
    pl.semaphore_wait(barrier, NC - 1 + len(greet))

    right, left = lax.rem(me + 1, NC), lax.rem(me + NC - 1, NC)
    to_right = pltpu.make_async_remote_copy(
        src_ref=g_ref.at[pl.ds(BF - 16, 16), :], dst_ref=halo_lo, send_sem=halo_send.at[0],
        recv_sem=halo_recv.at[0], device_id=(right, rec), device_id_type=MESH,
    )
    to_left = pltpu.make_async_remote_copy(
        src_ref=g_ref.at[pl.ds(0, 16), :], dst_ref=halo_hi, send_sem=halo_send.at[1],
        recv_sem=halo_recv.at[1], device_id=(left, rec), device_id_type=MESH,
    )
    to_right.start()
    to_left.start()
    for t in (TK, TV, TQ):
        each_peer(lambda d: remote(t, d).start())

    def to_partner(n, src, dst):
        return pltpu.make_async_remote_copy(
            src_ref=src, dst_ref=dst, send_sem=core_send.at[n], recv_sem=core_recv.at[n],
            device_id=partner, device_id_type=MESH,
        )

    def half(ref, base, c):
        return ref.at[:, pl.ds(mult(base + c * HALF, HALF), HALF)]

    group = {OUT: (dsub, 0), VAL: (dqkv, 2 * D), QUE: (dqkv, 0), KEY: (dqkv, D)}

    def swap_half(n):
        ref, base = group[n]
        return to_partner(n, half(ref, base, other), r2.at[theirs, pl.ds(n * HALF, HALF)])

    def own_half(n):
        ref, base = group[n]
        r2[mine, pl.ds(n * HALF, HALF)] = half(ref, base, core)[...]

    swap_li = to_partner(4, li_ref, li2.at[theirs, :])
    swap_att = to_partner(5, att2.at[mine, :], att2.at[theirs, :])
    swap_taps = to_partner(6, taps_c.at[core], taps_c.at[core])
    swap_li.start()

    length = len_ref[0]
    lane = lax.broadcasted_iota(jnp.int32, (BF, HD), 1)
    row = lax.broadcasted_iota(jnp.int32, (BF, HD), 0)

    def extra(d):
        masked = (lane == 0) & (row + origin(d) * BF >= length)
        k_aug[slot(d), pl.ds(HD, HD)] = jnp.where(masked, NEG, 0.0).astype(BF16)
        q_aug[slot(d), pl.ds(HD, HD)] = jnp.where(lane == 0, 1.0, 0.0).astype(BF16)
        v_aug[slot(d), pl.ds(HD, HD)] = jnp.where(lane < 2, 1.0, 0.0).astype(BF16)

    each_slot(extra)
    first = lax.broadcasted_iota(jnp.int32, (16, T), 0) == 0
    v_t[pl.ds(HD, 16), :] = jnp.where(first, 1.0, 0.0).astype(BF16)

    get_g.wait()
    gp[pl.ds(8, BF), :] = g_vm[...].astype(F32)
    to_right.wait_recv()
    to_left.wait_recv()
    low = halo_lo[...].astype(F32)[8:16, :]
    gp[pl.ds(0, 8), :] = jnp.where(me > 0, low, 0.0)
    high = halo_hi[...].astype(F32)[0:8, :]
    gp[pl.ds(8 + BF, 8), :] = jnp.where(me < NC - 1, high, 0.0)

    def conv_grad(n):
        cols = pl.ds(mult(n * HD, HD), HD)
        total = gp[pl.ds(8, BF), cols]
        for t in range(KW):
            total = total + conv_ref[pl.ds(t, 1), cols] * gp[pl.ds(12 - t, BF), cols]
        dsub[:, cols] = total.astype(BF16)

    each_slot(conv_grad)
    swap_half(OUT).start()
    own_half(OUT)
    get_wq.start()

    get_w.wait()

    def datt(d):
        rows = pl.ds(mult(peer(d) * HD, HD), HD)
        dat_s[d] = dot_nt(dsub[...], wout_vm[rows, :]).astype(BF16)

        @pl.when(d > 0)
        def _():
            remote(TD, d).start()

    each_slot(datt)
    local(TD).start()

    def turn_in(src, dst):
        def step(n, carry):
            cols = pl.ds(mult(n * BF, BF), BF)
            dst[cols, :] = src[:, cols].T
            return carry

        lax.fori_loop(0, D // BF, step, 0)

    get_li.wait()
    swap_li.wait_recv()
    turn_in(li2, li_t)

    for t in (TK, TV):
        local(t).wait()
        each_peer(lambda d: remote(t, d).wait_recv())

    def turn(d):
        k_t[:, slot(d)] = k_aug[slot(d), pl.ds(0, HD)].T
        v_t[pl.ds(0, HD), slot(d)] = v_aug[slot(d), pl.ds(0, HD)].T

    each_slot(turn)
    local(TQ).wait()

    def forward(d):
        @pl.when(d > 0)
        def _():
            remote(TQ, d).wait_recv()

        qd = q_aug[slot(d), :]
        top = None
        for b in range(T // KB):
            rows = pl.ds(b * KB, KB)
            s = dot_nt(k_aug[rows, :], qd)
            s_ref[rows, :] = s
            m = jnp.max(s, axis=0, keepdims=True)
            top = m if top is None else jnp.maximum(top, m)
        acc = jnp.zeros((HD + 16, BF), F32)
        for b in range(T // KB):
            rows = pl.ds(b * KB, KB)
            e = jnp.exp2((s_ref[rows, :] - top) * c_exp).astype(BF16)
            e_ref[rows, slot(d)] = e
            acc = acc + dot(v_t[:, rows], e)
        inv = 1.0 / acc[HD : HD + 1, :]
        att_s[d] = (acc[:HD, :] * inv).T.astype(BF16)
        linv_s[d] = jnp.broadcast_to(inv, (HD, BF)).T

        @pl.when(d > 0)
        def _():
            remote(BA, d).start()

    each_slot(forward)
    local(BA).start()

    local(TD).wait()

    def backward_in(d):
        @pl.when(d > 0)
        def _():
            remote(TD, d).wait_recv()

        do = (do_in[slot(d), :].astype(F32) * linv_s[d]).astype(BF16)
        delta = -jnp.sum(do.astype(F32) * att_s[d].astype(F32), axis=1, keepdims=True)
        hi = delta.astype(BF16).astype(F32)
        do_aug[slot(d), pl.ds(0, HD)] = do
        do_aug[slot(d), pl.ds(HD, HD)] = jnp.where(
            lane == 0, hi, jnp.where(lane == 1, delta - hi, 0.0)
        ).astype(BF16)

    each_slot(backward_in)

    def d_value(j):
        dv_s[j] = dot(e_ref[slot(j), :], do_aug[:, pl.ds(0, HD)]).astype(BF16)

        @pl.when(j > 0)
        def _():
            remote(BV, j).start()

    each_slot(d_value)
    local(BV).start()

    def d_query(d):
        dod = do_aug[slot(d), :]
        acc = jnp.zeros((HD, BF), F32)
        for b in range(T // KB):
            rows = pl.ds(b * KB, KB)
            dp = dot_nt(v_aug[rows, :], dod)
            ds = (e_ref[rows, slot(d)].astype(F32) * dp).astype(BF16)
            ds_ref[rows, slot(d)] = ds
            acc = acc + dot(k_t[:, rows], ds)
        dq_s[d] = (acc * inv_root).T.astype(BF16)

        @pl.when(d > 0)
        def _():
            remote(BQ, d).start()

    each_slot(d_query)
    local(BQ).start()

    def product(lhs, start, width):
        def step(b, carry):
            rows = pl.ds(mult(b * HD, HD), HD)
            g = dot(lhs[rows, :], r2[:, pl.ds(start, width)]).astype(BF16)
            grads[lax.div(b, 4), lax.rem(b, 4), :, :, :, pl.ds(start, width)] = g.reshape(
                2, 4, 16, width
            )
            return carry

        lax.fori_loop(0, D // HD, step, 0)

    def region(fixed, start, width):
        zl = zh = slice(None)
        if "z" in fixed:
            zl, zh = lax.rem(fixed["z"], 2), lax.div(fixed["z"], 2)
        return grads.at[
            zl, fixed.get("y", slice(None)), zh, fixed.get("x", slice(None)), :, pl.ds(start, width)
        ]

    class Stage:
        def __init__(self, part, stage):
            self.start, self.width, order = PARTS[part]
            self.axis = order[stage]
            self.fixed = {a: at[a] for a in order[:stage]}
            self.stage = stage

        def piece(self, by, start=0, width=None):
            width = self.width if width is None else width
            fixed = {**self.fixed, self.axis: off(self.axis, by)}
            return region(fixed, self.start + start, width)

        def copy(self, sems, n, src, dst, by):
            return pltpu.make_async_remote_copy(
                src_ref=src, dst_ref=dst, send_sem=sems[0].at[n], recv_sem=sems[1].at[n],
                device_id=device(self.axis, off(self.axis, by)), device_id_type=MESH,
            )

        def keep(self, total):
            if self.stage < 2:
                self.piece(0)[...] = total.astype(BF16)
            else:
                fin[:, pl.ds(self.start, self.width)] = total

        def sent(self):
            for c in self.copies:
                c.wait_send()

    class Ring(Stage):
        def __init__(self, part):
            super().__init__(part, 0)
            self.ra, self.rb, self.low, self.high = bufs[part * 6 : part * 6 + 4]
            h = self.width // 2
            lead = (slice(None),) * (len(self.low.shape) - 1)
            a, b = (*lead, pl.ds(0, h)), (*lead, pl.ds(h, h))
            ends = (
                (self.piece(2, 0, h), self.ra, 1),
                (self.piece(2, h, h), self.rb, 3),
                (self.piece(1, h, h), self.low.at[b], 1),
                (self.piece(3, 0, h), self.high.at[a], 3),
                (self.piece(1, 0, h), self.low.at[a], 1),
                (self.piece(3, h, h), self.high.at[b], 3),
            )
            sems = (ring_send, ring_recv)
            self.copies = [self.copy(sems, part * 6 + n, *e) for n, e in enumerate(ends)]

        def begin(self):
            for c in self.copies[:4]:
                c.start()

        def relay(self):
            h = self.width // 2
            for n, by, buf, start in ((0, 1, self.ra, 0), (1, 3, self.rb, h)):
                self.copies[n].wait_recv()
                here = self.piece(by, start, h)
                here[...] = (here[...].astype(F32) + buf[...].astype(F32)).astype(BF16)
                self.copies[4 + n].start()

        def end(self):
            for n in (2, 3, 4, 5):
                self.copies[n].wait_recv()
            here = self.piece(0)[...].astype(F32)
            self.keep(here + (self.low[...].astype(F32) + self.high[...].astype(F32)))

    class Direct(Stage):
        def __init__(self, part, stage):
            super().__init__(part, stage)
            self.buf = bufs[part * 6 + 3 + stage]
            base = (part * 2 + stage - 1) * 3
            sems = (step_send, step_recv)
            self.copies = [
                self.copy(sems, base + by - 1, self.piece(by), self.buf.at[by - 1], by)
                for by in (1, 2, 3)
            ]

        def begin(self):
            for c in self.copies:
                c.start()

        def end(self):
            for c in self.copies:
                c.wait_recv()
            here = self.piece(0)[...].astype(F32)
            b = [self.buf[n].astype(F32) for n in range(3)]
            self.keep((here + b[0]) + (b[1] + b[2]))

    rings = [(Ring(p), Direct(p, 1), Direct(p, 2)) for p in range(NP)]

    def arrived(t):
        local(t).wait()
        each_peer(lambda d: remote(t, d).wait_recv())

    def on(p, stage):
        rings[p][stage].end()
        rings[p][stage + 1].begin()

    taps_copies = []

    def taps_on(n, axis, value):
        taps_a[n, at[axis]] = value
        for by in (1, 2, 3):
            c = pltpu.make_async_remote_copy(
                src_ref=taps_a.at[n, at[axis]], dst_ref=taps_a.at[n, at[axis]],
                send_sem=taps_send.at[n * 3 + by - 1], recv_sem=taps_recv.at[n * 3 + by - 1],
                device_id=device(axis, off(axis, by)), device_id_type=MESH,
            )
            c.start()
            taps_copies.append(c)

    def taps_sum(n):
        for c in taps_copies[n * 3 :]:
            c.wait_recv()
        return (taps_a[n, 0] + taps_a[n, 1]) + (taps_a[n, 2] + taps_a[n, 3])

    arrived(BA)
    swap_att.start()
    swap_half(OUT).wait_recv()
    swap_att.wait_recv()
    turn_in(att2, att_t)
    product(att_t, OUT * HALF, HALF)
    rings[0][0].begin()

    def d_key(j):
        dk = dot(ds_ref[slot(j), :], q_aug[:, pl.ds(0, HD)])
        dk_s[j] = (dk * inv_root).astype(BF16)

        @pl.when(j > 0)
        def _():
            remote(BK, j).start()

    each_slot(d_key)
    local(BK).start()

    def taps(n):
        cols = pl.ds(mult(n * BF, BF), BF)
        sub = dot(att2[mine, :], wout_vm[:, cols]).astype(BF16).astype(F32)
        for t in range(KW):
            taps_c[core, pl.ds(t, 1), cols] = jnp.sum(
                sub * gp[pl.ds(12 - t, BF), cols], axis=0, keepdims=True
            )

    taps_c[core] = jnp.zeros((16, D), F32)
    lax.fori_loop(0, D // BF, lambda n, c: (taps(n), c)[1], 0)
    swap_taps.start()
    rings[0][0].relay()

    def weight(t, n):
        arrived(t)
        swap_half(n).start()
        own_half(n)
        swap_half(n).wait_recv()
        product(li_t, n * HALF, HALF)

    weight(BV, VAL)
    rings[1][0].begin()
    swap_taps.wait_recv()
    taps_on(0, "x", taps_c[0] + taps_c[1])
    weight(BQ, QUE)
    rings[2][0].begin()
    rings[3][0].begin()
    rings[1][0].relay()
    weight(BK, KEY)
    rings[4][0].begin()
    rings[5][0].begin()
    rings[2][0].relay()
    rings[3][0].relay()

    get_wq.wait()

    def d_input(n, carry):
        cols = pl.ds(mult(n * BF, BF), BF)
        din_vm[:, cols] = dot_nt(dqkv[...], wqkv_vm[cols, :]).astype(BF16)
        return carry

    lax.fori_loop(0, 2, d_input, 0)
    rings[4][0].relay()
    rings[5][0].relay()
    on(0, 0)
    taps_on(1, "y", taps_sum(0))
    lax.fori_loop(2, 4, d_input, 0)
    put_din = pltpu.make_async_copy(din_vm, din_out, local_sem.at[4])
    put_din.start()
    for p in (2, 3, 1, 4, 5):
        on(p, 0)
    on(0, 1)
    taps_on(2, "z", taps_sum(1))
    for p in (2, 3, 1, 4, 5):
        on(p, 1)
    dk_out[...] = taps_sum(2)[:KW]
    for p in range(NP):
        rings[p][2].end()

    last = to_partner(7, fin.at[pl.ds(mult(other * 8, 8), 8), :], fin_x)
    last.start()

    def place(block, who):
        for n, base in ((VAL, 2 * D), (QUE, 0), (KEY, D)):
            dwq_out[:, pl.ds(mult(base + who * HALF, HALF), HALF)] = block[
                :, n * HALF : (n + 1) * HALF
            ]
        dwo_out[:, pl.ds(mult(who * HALF, HALF), HALF)] = block[:, :HALF]

    place(fin[pl.ds(mult(core * 8, 8), 8), :], core)
    last.wait_recv()
    place(fin_x[...], other)

    put_din.wait()
    to_right.wait_send()
    to_left.wait_send()
    for t in range(8):
        each_peer(lambda d: remote(t, d).wait_send())
    for swap in (last, swap_li, swap_att, swap_taps, *(swap_half(n) for n in range(4))):
        swap.wait_send()
    for c in taps_copies:
        c.wait_send()
    for r in rings:
        for stage in r:
            stage.sent()


def collect_kernel(*refs):
    ins, outs, sems = refs[:4], refs[4:8], refs[8]
    copies = [pltpu.make_async_copy(a, b, sems.at[n]) for n, (a, b) in enumerate(zip(ins, outs))]
    for c in copies:
        c.start()
    for c in copies:
        c.wait()


def backward(lengths, li, q, k, v, g, conv, wout, wqkv):
    def vm(shape, dtype=BF16):
        return pltpu.VMEM(shape, dtype)

    buffers = []
    for _, width, order in PARTS:
        leads = []
        for stage in range(3):
            sizes = (("zl", 2), ("y", 4), ("zh", 2), ("x", 4))
            leads.append([n for axis, n in sizes if axis[0] not in order[: stage + 1]])
        for w in (width // 2, width // 2, width, width):
            buffers.append(vm((*leads[0], 16, w)))
        for stage in (1, 2):
            buffers.append(vm((3, *leads[stage], 16, width)))
    dma = pltpu.SemaphoreType.DMA
    outs = (
        jax.ShapeDtypeStruct((BF, D), BF16),
        jax.ShapeDtypeStruct((8, 3 * D), F32),
        jax.ShapeDtypeStruct((8, D), F32),
        jax.ShapeDtypeStruct((KW, D), F32),
    )
    results = pl.pallas_call(
        backward_kernel,
        out_shape=outs,
        in_specs=[pl.BlockSpec(memory_space=pltpu.SMEM), ANY, ANY, ANY, ANY, ANY, VM, ANY, ANY],
        out_specs=(ANY, VM, VM, VM),
        scratch_shapes=[
            vm((T, 2 * HD)), vm((T, 2 * HD)), vm((T, 2 * HD)), vm((T, HD)), vm((T, 2 * HD)),
            vm((HD, T)), vm((HD + 16, T)), vm((T, BF), F32), vm((T, T)), vm((T, T)),
            vm((NC, BF, HD)), vm((NC, BF, HD), F32), vm((NC, BF, HD)), vm((NC, BF, HD)),
            vm((NC, BF, HD)), vm((NC, BF, HD)), vm((BF, 3 * D)), vm((BF, D)),
            vm((BF, D)), vm((BF + 16, D), F32), vm((BF, D)), vm((16, D)), vm((16, D)),
            vm((D, D)), vm((D, 3 * D)),
            vm((2 * BF, D)), vm((2 * BF, D)), vm((2 * BF, CW)), vm((D, 2 * BF)), vm((D, 2 * BF)),
            vm((2, 4, 2, 4, 16, CW)), vm((16, CW), F32), vm((8, CW), F32),
            vm((2, 16, D), F32), vm((3, 4, 16, D), F32), *buffers,
            dma((8, NC)), dma((8, NC)), dma((2,)), dma((2,)), dma((5,)), dma((8,)), dma((8,)),
            dma((NP * 6,)), dma((NP * 6,)), dma((NP * 6,)), dma((NP * 6,)), dma((9,)), dma((9,)),
        ],
        compiler_params=pltpu.CompilerParams(
            collective_id=0, has_side_effects=True, vmem_limit_bytes=60 * 1024 * 1024
        ),
    )(lengths, li, q, k, v, g, conv, wout, wqkv)
    return pl.pallas_call(
        collect_kernel,
        out_shape=outs,
        in_specs=[ANY] * 4,
        out_specs=(ANY,) * 4,
        scratch_shapes=[dma((4,))],
    )(*results)


def shards(layer_in, queries, keys, values, lengths, w_qkv, w_out, conv_kernel, grad_out):
    d_input, d_wqkv, d_wout, d_kernel = backward(
        lengths, layer_in[0], queries[0], keys[0], values[0], grad_out[0], conv_kernel, w_out, w_qkv
    )
    return d_input[None], d_wqkv, d_wout, d_kernel


def solution(mesh):
    frames = P("rec", "ctx", None)
    in_specs = (frames, frames, frames, frames, P("rec"), P(), P(), P(), frames)
    out_specs = (frames, P(("ctx", "rec"), None), P(("ctx", "rec"), None), P())
    return jax.shard_map(
        shards, mesh=mesh, in_specs=in_specs, out_specs=out_specs, check_vma=False
    )
```

time: 125 us -> 119 us (0.952)
  local copies, waits for them, and re-layouts: 6.25 us -> 0 us
    unnamed x4 -> x0, local copies, waits for them, and re-layouts: 6.25 us -> none
where the time goes in v2:
time: 119 us
  Pallas kernels  118 us (99%)
  between operations  1.29 us (1%)
    pallas_call x1, Pallas kernels, backward(): pl.pallas_call(backward_kernel, out_shape=outs, in_specs=[pl.BlockSpec(me...  94.9 us
    pallas_call x1, Pallas kernels, backward(): pl.pallas_call(collect_kernel, out_shape=outs, in_specs=[ANY] * 4, out_sp...  23 us

profile of v2, /device:TPU:1, one launch (start us, length us, event | category | flops | bytes accessed | tf_op | source)
XLA Modules:
  0.0 119.2 jit_solution(9643528380994954140)
XLA Ops:
  1.3 94.9 %shard_map.120 = (bf16[256,1024]{1,0:T(8,128)(2,1)}, f32[8,3072]{1,0:T(8,128)}, f32[8,1024]{1,0:T(8,128)}, f32[9,1024]{1,0:T(8,128)}) custom-call(s32[1]{0:T(128)S(6)} %copy.13.len_ref, bf16[256,1024]{1,0:T(8,128)(2,1)} %bitcast.6, bf16[256,1024]{1,0:T(8,128)(2,1)} %bitcast.7, bf16[256,1024]{1,0:T(8,128)(2,1)} %bitcast.8, bf16[256,1024]{1,0:T(8,128)(2,1)} %bitcast.9, ...), custom_call_target="tpu_custom_call" | custom-call | tf_op jit(solution)/shard_map/pallas_call | solution.py:618
  96.2 23.0 %shard_map.121 = (bf16[256,1024]{1,0:T(8,128)(2,1)}, f32[8,3072]{1,0:T(8,128)}, f32[8,1024]{1,0:T(8,128)}, f32[9,1024]{1,0:T(8,128)}) custom-call(bf16[256,1024]{1,0:T(8,128)(2,1)} %get-tuple-element.12.refs_0_, f32[8,3072]{1,0:T(8,128)} %get-tuple-element.13.refs_1_, f32[8,1024]{1,0:T(8,128)} %get-tuple-element.14.refs_2_, f32[9,1024]{1,0:T(8,128)} %get-tuple-element.15.refs_3_), custom_call_target="tpu_custom_call" | custom-call | tf_op jit(solution)/shard_map/pallas_call | solution.py:640

commit v3 on v2

--- a/solution.py
+++ b/solution.py
@@ -45,10 +45,12 @@
     (512, 512, ("x", "z", "y")),
     (1024, 256, ("y", "z", "x")),
     (1280, 256, ("z", "y", "x")),
-    (1536, 256, ("y", "x", "z")),
-    (1792, 256, ("z", "x", "y")),
+    (1536, 256, ("x", "y", "z")),
+    (1792, 128, ("y", "z", "x")),
+    (1920, 128, ("z", "x", "y")),
 )
 NP = len(PARTS)
+NR = 4
 
 
 def backward_kernel(
@@ -57,11 +59,12 @@
     q_aug, k_aug, v_aug, do_in, do_aug, k_t, v_t, s_ref, e_ref, ds_ref,
     att_s, linv_s, dq_s, dk_s, dv_s, dat_s, dqkv, din_vm,
     g_vm, gp, dsub, halo_lo, halo_hi, wout_vm, wqkv_vm,
-    li2, att2, r2, li_t, att_t, grads, fin, fin_x, taps_c, taps_a, *rest,
+    li2, att2, r2, li_t, att_t, grads, taps_c, taps_a, *rest,
 ):
-    bufs = rest[: NP * 6]
+    bufs = rest[: NP * 7]
     (send_sem, recv_sem, halo_send, halo_recv, local_sem, core_send, core_recv,
-     ring_send, ring_recv, step_send, step_recv, taps_send, taps_recv) = rest[NP * 6 :]
+     ring_send, ring_recv, step_send, step_recv, last_send, last_recv,
+     taps_send, taps_recv) = rest[NP * 7 :]
     me = lax.axis_index("ctx")
     rec = lax.axis_index("rec")
     z, y = lax.div(me, 4), lax.rem(me, 4)
@@ -128,7 +131,7 @@
     get_w = pltpu.make_async_copy(wout_ref, wout_vm, local_sem.at[1])
     get_g.start()
     get_w.start()
-    for t in (TK, TV, TQ):
+    for t in (TK, TQ, TV):
         local(t).start()
     mine, theirs = pl.ds(0, BF), pl.ds(BF, BF)
     get_li = pltpu.make_async_copy(li_ref, li2.at[mine, :], local_sem.at[2])
@@ -153,6 +156,7 @@
     far = lax.rem(lax.div(rec, 8) + 1, 2)
     greet = [partner] + [device("x", off("x", by)) for by in (1, 2, 3)]
     greet += [device("z", far * 2 + zl) for zl in (0, 1)]
+    greet += [device(a, off(a, by), other) for a in "xyz" for by in (1, 2, 3)]
 
     barrier = pltpu.get_barrier_semaphore()
     each_peer(
@@ -173,7 +177,7 @@
     )
     to_right.start()
     to_left.start()
-    for t in (TK, TV, TQ):
+    for t in (TK, TQ, TV):
         each_peer(lambda d: remote(t, d).start())
 
     def to_partner(n, src, dst):
@@ -260,18 +264,14 @@
     swap_li.wait_recv()
     turn_in(li2, li_t)
 
-    for t in (TK, TV):
+    def arrived(t):
         local(t).wait()
         each_peer(lambda d: remote(t, d).wait_recv())
 
-    def turn(d):
-        k_t[:, slot(d)] = k_aug[slot(d), pl.ds(0, HD)].T
-        v_t[pl.ds(0, HD), slot(d)] = v_aug[slot(d), pl.ds(0, HD)].T
-
-    each_slot(turn)
+    arrived(TK)
     local(TQ).wait()
 
-    def forward(d):
+    def scores(d):
         @pl.when(d > 0)
         def _():
             remote(TQ, d).wait_recv()
@@ -284,12 +284,21 @@
             s_ref[rows, :] = s
             m = jnp.max(s, axis=0, keepdims=True)
             top = m if top is None else jnp.maximum(top, m)
-        acc = jnp.zeros((HD + 16, BF), F32)
         for b in range(T // KB):
             rows = pl.ds(b * KB, KB)
-            e = jnp.exp2((s_ref[rows, :] - top) * c_exp).astype(BF16)
-            e_ref[rows, slot(d)] = e
-            acc = acc + dot(v_t[:, rows], e)
+            e_ref[rows, slot(d)] = jnp.exp2((s_ref[rows, :] - top) * c_exp).astype(BF16)
+
+    each_slot(scores)
+    arrived(TV)
+
+    def turn(d):
+        k_t[:, slot(d)] = k_aug[slot(d), pl.ds(0, HD)].T
+        v_t[pl.ds(0, HD), slot(d)] = v_aug[slot(d), pl.ds(0, HD)].T
+
+    each_slot(turn)
+
+    def attend(d):
+        acc = dot(v_t[...], e_ref[:, slot(d)])
         inv = 1.0 / acc[HD : HD + 1, :]
         att_s[d] = (acc[:HD, :] * inv).T.astype(BF16)
         linv_s[d] = jnp.broadcast_to(inv, (HD, BF)).T
@@ -298,7 +307,7 @@
         def _():
             remote(BA, d).start()
 
-    each_slot(forward)
+    each_slot(attend)
     local(BA).start()
 
     local(TD).wait()
@@ -319,13 +328,16 @@
     each_slot(backward_in)
 
     def d_value(j):
-        dv_s[j] = dot(e_ref[slot(j), :], do_aug[:, pl.ds(0, HD)]).astype(BF16)
+        two = pl.ds(mult(j * 2 * BF, 2 * BF), 2 * BF)
+        dv_s[pl.ds(j * 2, 2)] = dot(e_ref[two, :], do_aug[:, pl.ds(0, HD)]).astype(BF16).reshape(2, BF, HD)
 
         @pl.when(j > 0)
         def _():
-            remote(BV, j).start()
-
-    each_slot(d_value)
+            remote(BV, j * 2).start()
+
+        remote(BV, j * 2 + 1).start()
+
+    lax.fori_loop(0, NC // 2, lambda j, c: (d_value(j), c)[1], 0)
     local(BV).start()
 
     def d_query(d):
@@ -347,15 +359,13 @@
     local(BQ).start()
 
     def product(lhs, start, width):
-        def step(b, carry):
-            rows = pl.ds(mult(b * HD, HD), HD)
+        def step(zl, carry):
+            rows = pl.ds(mult(zl * HALF, HALF), HALF)
             g = dot(lhs[rows, :], r2[:, pl.ds(start, width)]).astype(BF16)
-            grads[lax.div(b, 4), lax.rem(b, 4), :, :, :, pl.ds(start, width)] = g.reshape(
-                2, 4, 16, width
-            )
+            grads[zl, :, :, :, :, pl.ds(start, width)] = g.reshape(4, 2, 4, 16, width)
             return carry
 
-        lax.fori_loop(0, D // HD, step, 0)
+        lax.fori_loop(0, 2, step, 0)
 
     def region(fixed, start, width):
         zl = zh = slice(None)
@@ -368,6 +378,7 @@
     class Stage:
         def __init__(self, part, stage):
             self.start, self.width, order = PARTS[part]
+            self.part = part
             self.axis = order[stage]
             self.fixed = {a: at[a] for a in order[:stage]}
             self.stage = stage
@@ -384,10 +395,12 @@
             )
 
         def keep(self, total):
-            if self.stage < 2:
+            if self.stage == 0:
                 self.piece(0)[...] = total.astype(BF16)
             else:
-                fin[:, pl.ds(self.start, self.width)] = total
+                pair = bufs[self.part * 7 + 5]
+                pair[..., 0, :, :] = total[..., :8, :]
+                pair[..., 1, :, :] = total[..., 8:, :]
 
         def sent(self):
             for c in self.copies:
@@ -396,7 +409,7 @@
     class Ring(Stage):
         def __init__(self, part):
             super().__init__(part, 0)
-            self.ra, self.rb, self.low, self.high = bufs[part * 6 : part * 6 + 4]
+            self.ra, self.rb, self.low, self.high = bufs[part * 7 : part * 7 + 4]
             h = self.width // 2
             lead = (slice(None),) * (len(self.low.shape) - 1)
             a, b = (*lead, pl.ds(0, h)), (*lead, pl.ds(h, h))
@@ -432,8 +445,8 @@
     class Direct(Stage):
         def __init__(self, part, stage):
             super().__init__(part, stage)
-            self.buf = bufs[part * 6 + 3 + stage]
-            base = (part * 2 + stage - 1) * 3
+            self.buf = bufs[part * 7 + 3 + stage] if stage else bufs[part * 7]
+            base = (part * 2 + stage) * 3
             sems = (step_send, step_recv)
             self.copies = [
                 self.copy(sems, base + by - 1, self.piece(by), self.buf.at[by - 1], by)
@@ -451,11 +464,47 @@
             b = [self.buf[n].astype(F32) for n in range(3)]
             self.keep((here + b[0]) + (b[1] + b[2]))
 
-    rings = [(Ring(p), Direct(p, 1), Direct(p, 2)) for p in range(NP)]
-
-    def arrived(t):
-        local(t).wait()
-        each_peer(lambda d: remote(t, d).wait_recv())
+    class Last(Stage):
+        def __init__(self, part):
+            super().__init__(part, 2)
+            self.pair, self.buf = bufs[part * 7 + 5 : part * 7 + 7]
+            self.copies = []
+            for n, (turned, by) in enumerate((t, b) for t in (0, 1) for b in range(4) if t + b):
+                to = lax.rem(core + turned, 2)
+                who = device(self.axis, off(self.axis, by), to)
+                self.copies.append(
+                    pltpu.make_async_remote_copy(
+                        src_ref=self.rows(by, to), dst_ref=self.buf.at[n],
+                        send_sem=last_send.at[part * 7 + n], recv_sem=last_recv.at[part * 7 + n],
+                        device_id=who, device_id_type=MESH,
+                    )
+                )
+
+        def rows(self, by, to):
+            chip = off(self.axis, by)
+            if self.axis == "z":
+                return self.pair.at[lax.rem(chip, 2), lax.div(chip, 2), to]
+            return self.pair.at[chip, to]
+
+        def begin(self):
+            for c in self.copies:
+                c.start()
+
+        def end(self):
+            for c in self.copies:
+                c.wait_recv()
+            b = [self.buf[n] for n in range(7)]
+            here = self.rows(0, core)[...]
+            n, inside = divmod(self.start, HALF)
+            out, base = ((dwo_out, 0), (dwq_out, 2 * D), (dwq_out, 0), (dwq_out, D))[n]
+            for who, block in (
+                (core, (here + b[0]) + (b[1] + b[2])),
+                (other, (b[3] + b[4]) + (b[5] + b[6])),
+            ):
+                cols = pl.ds(mult(base + who * HALF + inside, HD), self.width)
+                out[:, cols] = block
+
+    rings = [(Ring(p) if p < NR else Direct(p, 0), Direct(p, 1), Last(p)) for p in range(NP)]
 
     def on(p, stage):
         rings[p][stage].end()
@@ -481,22 +530,25 @@
 
     arrived(BA)
     swap_att.start()
+
+    def d_key(j):
+        two = pl.ds(mult(j * 2 * BF, 2 * BF), 2 * BF)
+        dk_s[pl.ds(j * 2, 2)] = (dot(ds_ref[two, :], q_aug[:, pl.ds(0, HD)]) * inv_root).astype(BF16).reshape(2, BF, HD)
+
+        @pl.when(j > 0)
+        def _():
+            remote(BK, j * 2).start()
+
+        remote(BK, j * 2 + 1).start()
+
+    lax.fori_loop(0, NC // 2, lambda j, c: (d_key(j), c)[1], 0)
+    local(BK).start()
+
     swap_half(OUT).wait_recv()
     swap_att.wait_recv()
     turn_in(att2, att_t)
     product(att_t, OUT * HALF, HALF)
     rings[0][0].begin()
-
-    def d_key(j):
-        dk = dot(ds_ref[slot(j), :], q_aug[:, pl.ds(0, HD)])
-        dk_s[j] = (dk * inv_root).astype(BF16)
-
-        @pl.when(j > 0)
-        def _():
-            remote(BK, j).start()
-
-    each_slot(d_key)
-    local(BK).start()
 
     def taps(n):
         cols = pl.ds(mult(n * BF, BF), BF)
@@ -506,77 +558,64 @@
                 sub * gp[pl.ds(12 - t, BF), cols], axis=0, keepdims=True
             )
 
-    taps_c[core] = jnp.zeros((16, D), F32)
-    lax.fori_loop(0, D // BF, lambda n, c: (taps(n), c)[1], 0)
-    swap_taps.start()
-    rings[0][0].relay()
-
-    def weight(t, n):
+    def back(t, n):
         arrived(t)
         swap_half(n).start()
         own_half(n)
+
+    def weight(n):
         swap_half(n).wait_recv()
         product(li_t, n * HALF, HALF)
-
-    weight(BV, VAL)
-    rings[1][0].begin()
-    swap_taps.wait_recv()
-    taps_on(0, "x", taps_c[0] + taps_c[1])
-    weight(BQ, QUE)
-    rings[2][0].begin()
-    rings[3][0].begin()
-    rings[1][0].relay()
-    weight(BK, KEY)
-    rings[4][0].begin()
-    rings[5][0].begin()
-    rings[2][0].relay()
-    rings[3][0].relay()
-
-    get_wq.wait()
 
     def d_input(n, carry):
         cols = pl.ds(mult(n * BF, BF), BF)
         din_vm[:, cols] = dot_nt(dqkv[...], wqkv_vm[cols, :]).astype(BF16)
         return carry
 
-    lax.fori_loop(0, 2, d_input, 0)
-    rings[4][0].relay()
-    rings[5][0].relay()
+    taps_c[core] = jnp.zeros((16, D), F32)
+    lax.fori_loop(0, D // BF, lambda n, c: (taps(n), c)[1], 0)
+    swap_taps.start()
+    back(BV, VAL)
+    rings[0][0].relay()
+    weight(VAL)
+    rings[1][0].begin()
+    swap_taps.wait_recv()
+    taps_on(0, "x", taps_c[0] + taps_c[1])
+    back(BQ, QUE)
+    get_wq.wait()
+    weight(QUE)
+    rings[2][0].begin()
+    rings[3][0].begin()
+    rings[1][0].relay()
     on(0, 0)
     taps_on(1, "y", taps_sum(0))
+    back(BK, KEY)
+    lax.fori_loop(0, 2, d_input, 0)
+    weight(KEY)
+    for p in (4, 5, 6):
+        rings[p][0].begin()
+    rings[2][0].relay()
+    rings[3][0].relay()
     lax.fori_loop(2, 4, d_input, 0)
     put_din = pltpu.make_async_copy(din_vm, din_out, local_sem.at[4])
     put_din.start()
-    for p in (2, 3, 1, 4, 5):
-        on(p, 0)
+    on(1, 0)
     on(0, 1)
     taps_on(2, "z", taps_sum(1))
-    for p in (2, 3, 1, 4, 5):
+    for p in (2, 3, 4, 5, 6):
+        on(p, 0)
+    for p in (1, 2, 3, 4, 5, 6):
         on(p, 1)
     dk_out[...] = taps_sum(2)[:KW]
     for p in range(NP):
         rings[p][2].end()
-
-    last = to_partner(7, fin.at[pl.ds(mult(other * 8, 8), 8), :], fin_x)
-    last.start()
-
-    def place(block, who):
-        for n, base in ((VAL, 2 * D), (QUE, 0), (KEY, D)):
-            dwq_out[:, pl.ds(mult(base + who * HALF, HALF), HALF)] = block[
-                :, n * HALF : (n + 1) * HALF
-            ]
-        dwo_out[:, pl.ds(mult(who * HALF, HALF), HALF)] = block[:, :HALF]
-
-    place(fin[pl.ds(mult(core * 8, 8), 8), :], core)
-    last.wait_recv()
-    place(fin_x[...], other)
 
     put_din.wait()
     to_right.wait_send()
     to_left.wait_send()
     for t in range(8):
         each_peer(lambda d: remote(t, d).wait_send())
-    for swap in (last, swap_li, swap_att, swap_taps, *(swap_half(n) for n in range(4))):
+    for swap in (swap_li, swap_att, swap_taps, *(swap_half(n) for n in range(4))):
         swap.wait_send()
     for c in taps_copies:
         c.wait_send()
@@ -586,12 +625,8 @@
 
 
 def collect_kernel(*refs):
-    ins, outs, sems = refs[:4], refs[4:8], refs[8]
-    copies = [pltpu.make_async_copy(a, b, sems.at[n]) for n, (a, b) in enumerate(zip(ins, outs))]
-    for c in copies:
-        c.start()
-    for c in copies:
-        c.wait()
+    for a, b in zip(refs[:4], refs[4:]):
+        b[...] = a[...]
 
 
 def backward(lengths, li, q, k, v, g, conv, wout, wqkv):
@@ -599,15 +634,19 @@
         return pltpu.VMEM(shape, dtype)
 
     buffers = []
-    for _, width, order in PARTS:
+    for p, (_, width, order) in enumerate(PARTS):
         leads = []
         for stage in range(3):
             sizes = (("zl", 2), ("y", 4), ("zh", 2), ("x", 4))
             leads.append([n for axis, n in sizes if axis[0] not in order[: stage + 1]])
-        for w in (width // 2, width // 2, width, width):
-            buffers.append(vm((*leads[0], 16, w)))
-        for stage in (1, 2):
-            buffers.append(vm((3, *leads[stage], 16, width)))
+        if p < NR:
+            first = [(*leads[0], 16, w) for w in (width // 2, width // 2, width, width)]
+        else:
+            first = [(3, *leads[0], 16, width)] + [(16, HD)] * 3
+        buffers += [vm(shape) for shape in first]
+        buffers.append(vm((3, *leads[1], 16, width)))
+        buffers.append(vm((*leads[1], 2, 8, width), F32))
+        buffers.append(vm((7, 8, width), F32))
     dma = pltpu.SemaphoreType.DMA
     outs = (
         jax.ShapeDtypeStruct((BF, D), BF16),
@@ -628,10 +667,11 @@
             vm((BF, D)), vm((BF + 16, D), F32), vm((BF, D)), vm((16, D)), vm((16, D)),
             vm((D, D)), vm((D, 3 * D)),
             vm((2 * BF, D)), vm((2 * BF, D)), vm((2 * BF, CW)), vm((D, 2 * BF)), vm((D, 2 * BF)),
-            vm((2, 4, 2, 4, 16, CW)), vm((16, CW), F32), vm((8, CW), F32),
+            vm((2, 4, 2, 4, 16, CW)),
             vm((2, 16, D), F32), vm((3, 4, 16, D), F32), *buffers,
             dma((8, NC)), dma((8, NC)), dma((2,)), dma((2,)), dma((5,)), dma((8,)), dma((8,)),
-            dma((NP * 6,)), dma((NP * 6,)), dma((NP * 6,)), dma((NP * 6,)), dma((9,)), dma((9,)),
+            dma((NR * 6,)), dma((NR * 6,)), dma((NP * 6,)), dma((NP * 6,)),
+            dma((NP * 7,)), dma((NP * 7,)), dma((9,)), dma((9,)),
         ],
         compiler_params=pltpu.CompilerParams(
             collective_id=0, has_side_effects=True, vmem_limit_bytes=60 * 1024 * 1024
@@ -640,9 +680,8 @@
     return pl.pallas_call(
         collect_kernel,
         out_shape=outs,
-        in_specs=[ANY] * 4,
-        out_specs=(ANY,) * 4,
-        scratch_shapes=[dma((4,))],
+        in_specs=[VM] * 4,
+        out_specs=(VM,) * 4,
     )(*results)
 
 

time: 119 us -> 102 us (0.86)
  Pallas kernels: 118 us -> 101 us
    pallas_call x1, Pallas kernels: 23 us -> 1.96 us  [backward(): pl.pallas_call(collect_kernel, out_shape=outs, in_specs=[VM] * 4, out_spe...]
    pallas_call x1, Pallas kernels: 94.9 us -> 99 us  [backward(): pl.pallas_call(backward_kernel, out_shape=outs, in_specs=[pl.BlockSpec(me...]
where the time goes in v3:
time: 102 us
  Pallas kernels  101 us (99%)
  between operations  1.29 us (1%)
    pallas_call x1, Pallas kernels, backward(): pl.pallas_call(backward_kernel, out_shape=outs, in_specs=[pl.BlockSpec(me...  99 us

profile of v3, /device:TPU:1, one launch (start us, length us, event | category | flops | bytes accessed | tf_op | source)
XLA Modules:
  0.0 102.2 jit_solution(7041029959283055350)
XLA Ops:
  1.3 99.0 %shard_map.120 = (bf16[256,1024]{1,0:T(8,128)(2,1)}, f32[8,3072]{1,0:T(8,128)}, f32[8,1024]{1,0:T(8,128)}, f32[9,1024]{1,0:T(8,128)}) custom-call(s32[1]{0:T(128)S(6)} %copy.13.len_ref, bf16[256,1024]{1,0:T(8,128)(2,1)} %bitcast.6, bf16[256,1024]{1,0:T(8,128)(2,1)} %bitcast.7, bf16[256,1024]{1,0:T(8,128)(2,1)} %bitcast.8, bf16[256,1024]{1,0:T(8,128)(2,1)} %bitcast.9, ...), custom_call_target="tpu_custom_call" | custom-call | tf_op jit(solution)/shard_map/pallas_call | solution.py:657
  100.3 2.0 %shard_map.121 = (bf16[256,1024]{1,0:T(8,128)(2,1)}, f32[8,3072]{1,0:T(8,128)}, f32[8,1024]{1,0:T(8,128)}, f32[9,1024]{1,0:T(8,128)}) custom-call(bf16[256,1024]{1,0:T(8,128)(2,1)} %get-tuple-element.12.refs_0_, f32[8,3072]{1,0:T(8,128)} %get-tuple-element.13.refs_1_, f32[8,1024]{1,0:T(8,128)} %get-tuple-element.14.refs_2_, f32[9,1024]{1,0:T(8,128)} %get-tuple-element.15.refs_3_), custom_call_target="tpu_custom_call" | custom-call | tf_op jit(solution)/shard_map/pallas_call | solution.py:680

commit v4 on v3

--- a/solution.py
+++ b/solution.py
@@ -43,23 +43,22 @@
 PARTS = (
     (0, 512, ("x", "y", "z")),
     (512, 512, ("x", "z", "y")),
-    (1024, 256, ("y", "z", "x")),
-    (1280, 256, ("z", "y", "x")),
-    (1536, 256, ("x", "y", "z")),
-    (1792, 128, ("y", "z", "x")),
-    (1920, 128, ("z", "x", "y")),
+    (1024, 256, ("y", "x", "z")),
+    (1280, 256, ("z", "x", "y")),
+    (1536, 256, ("y", "z", "x")),
+    (1792, 256, ("z", "y", "x")),
 )
 NP = len(PARTS)
-NR = 4
+NR = 6
 
 
 def backward_kernel(
     len_ref, li_ref, q_ref, k_ref, v_ref, g_ref, conv_ref, wout_ref, wqkv_ref,
-    din_out, dwq_out, dwo_out, dk_out,
+    din_hbm, dwq_hbm, dwo_hbm, dk_hbm,
     q_aug, k_aug, v_aug, do_in, do_aug, k_t, v_t, s_ref, e_ref, ds_ref,
     att_s, linv_s, dq_s, dk_s, dv_s, dat_s, dqkv, din_vm,
     g_vm, gp, dsub, halo_lo, halo_hi, wout_vm, wqkv_vm,
-    li2, att2, r2, li_t, att_t, grads, taps_c, taps_a, *rest,
+    li2, att2, r2, li_t, att_t, grads, taps_c, taps_a, conv_vm, dwq_out, dwo_out, dk_out, *rest,
 ):
     bufs = rest[: NP * 7]
     (send_sem, recv_sem, halo_send, halo_recv, local_sem, core_send, core_recv,
@@ -137,6 +136,8 @@
     get_li = pltpu.make_async_copy(li_ref, li2.at[mine, :], local_sem.at[2])
     get_li.start()
     get_wq = pltpu.make_async_copy(wqkv_ref, wqkv_vm, local_sem.at[3])
+    get_conv = pltpu.make_async_copy(conv_ref, conv_vm, local_sem.at[5])
+    get_conv.start()
 
     core = lax.rem(rec, 2)
     other = 1 - core
@@ -219,6 +220,7 @@
     v_t[pl.ds(HD, 16), :] = jnp.where(first, 1.0, 0.0).astype(BF16)
 
     get_g.wait()
+    get_conv.wait()
     gp[pl.ds(8, BF), :] = g_vm[...].astype(F32)
     to_right.wait_recv()
     to_left.wait_recv()
@@ -231,7 +233,7 @@
         cols = pl.ds(mult(n * HD, HD), HD)
         total = gp[pl.ds(8, BF), cols]
         for t in range(KW):
-            total = total + conv_ref[pl.ds(t, 1), cols] * gp[pl.ds(12 - t, BF), cols]
+            total = total + conv_vm[pl.ds(t, 1), cols] * gp[pl.ds(12 - t, BF), cols]
         dsub[:, cols] = total.astype(BF16)
 
     each_slot(conv_grad)
@@ -355,7 +357,10 @@
         def _():
             remote(BQ, d).start()
 
-    each_slot(d_query)
+    lax.fori_loop(0, 5, lambda d, c: (d_query(d), c)[1], 0)
+    arrived(BA)
+    swap_att.start()
+    lax.fori_loop(5, NC, lambda d, c: (d_query(d), c)[1], 0)
     local(BQ).start()
 
     def product(lhs, start, width):
@@ -528,27 +533,24 @@
             c.wait_recv()
         return (taps_a[n, 0] + taps_a[n, 1]) + (taps_a[n, 2] + taps_a[n, 3])
 
-    arrived(BA)
-    swap_att.start()
-
-    def d_key(j):
-        two = pl.ds(mult(j * 2 * BF, 2 * BF), 2 * BF)
-        dk_s[pl.ds(j * 2, 2)] = (dot(ds_ref[two, :], q_aug[:, pl.ds(0, HD)]) * inv_root).astype(BF16).reshape(2, BF, HD)
-
-        @pl.when(j > 0)
-        def _():
-            remote(BK, j * 2).start()
-
-        remote(BK, j * 2 + 1).start()
-
-    lax.fori_loop(0, NC // 2, lambda j, c: (d_key(j), c)[1], 0)
-    local(BK).start()
-
     swap_half(OUT).wait_recv()
     swap_att.wait_recv()
     turn_in(att2, att_t)
     product(att_t, OUT * HALF, HALF)
     rings[0][0].begin()
+
+    def d_key(j):
+        two = pl.ds(mult(j * 2 * BF, 2 * BF), 2 * BF)
+        dk_s[pl.ds(j * 2, 2)] = (dot(ds_ref[two, :], q_aug[:, pl.ds(0, HD)]) * inv_root).astype(BF16).reshape(2, BF, HD)
+
+        @pl.when(j > 0)
+        def _():
+            remote(BK, j * 2).start()
+
+        remote(BK, j * 2 + 1).start()
+
+    lax.fori_loop(0, NC // 2, lambda j, c: (d_key(j), c)[1], 0)
+    local(BK).start()
 
     def taps(n):
         cols = pl.ds(mult(n * BF, BF), BF)
@@ -572,45 +574,50 @@
         din_vm[:, cols] = dot_nt(dqkv[...], wqkv_vm[cols, :]).astype(BF16)
         return carry
 
+    back(BV, VAL)
+    rings[0][0].relay()
     taps_c[core] = jnp.zeros((16, D), F32)
     lax.fori_loop(0, D // BF, lambda n, c: (taps(n), c)[1], 0)
     swap_taps.start()
-    back(BV, VAL)
-    rings[0][0].relay()
     weight(VAL)
     rings[1][0].begin()
+    back(BQ, QUE)
+    get_wq.wait()
     swap_taps.wait_recv()
     taps_on(0, "x", taps_c[0] + taps_c[1])
-    back(BQ, QUE)
-    get_wq.wait()
     weight(QUE)
     rings[2][0].begin()
     rings[3][0].begin()
-    rings[1][0].relay()
-    on(0, 0)
-    taps_on(1, "y", taps_sum(0))
     back(BK, KEY)
     lax.fori_loop(0, 2, d_input, 0)
     weight(KEY)
-    for p in (4, 5, 6):
-        rings[p][0].begin()
+    rings[4][0].begin()
+    rings[5][0].begin()
+    rings[1][0].relay()
     rings[2][0].relay()
     rings[3][0].relay()
+    on(0, 0)
+    rings[4][0].relay()
+    rings[5][0].relay()
     lax.fori_loop(2, 4, d_input, 0)
-    put_din = pltpu.make_async_copy(din_vm, din_out, local_sem.at[4])
+    put_din = pltpu.make_async_copy(din_vm, din_hbm, local_sem.at[4])
     put_din.start()
+    taps_on(1, "y", taps_sum(0))
+    on(2, 0)
+    on(3, 0)
+    on(0, 1)
     on(1, 0)
-    on(0, 1)
+    on(4, 0)
+    on(5, 0)
     taps_on(2, "z", taps_sum(1))
-    for p in (2, 3, 4, 5, 6):
-        on(p, 0)
-    for p in (1, 2, 3, 4, 5, 6):
+    for p in (2, 3, 1, 4, 5):
         on(p, 1)
     dk_out[...] = taps_sum(2)[:KW]
-    for p in range(NP):
-        rings[p][2].end()
-
-    put_din.wait()
+    puts = [
+        pltpu.make_async_copy(a, b, local_sem.at[n])
+        for a, b, n in ((dk_out, dk_hbm, 6), (dwo_out, dwo_hbm, 7), (dwq_out, dwq_hbm, 8))
+    ]
+    puts[0].start()
     to_right.wait_send()
     to_left.wait_send()
     for t in range(8):
@@ -620,8 +627,18 @@
     for c in taps_copies:
         c.wait_send()
     for r in rings:
-        for stage in r:
-            stage.sent()
+        r[0].sent()
+        r[1].sent()
+    rings[0][2].end()
+    puts[1].start()
+    for p in range(1, NP):
+        rings[p][2].end()
+    puts[2].start()
+    for r in rings:
+        r[2].sent()
+    put_din.wait()
+    for put in puts:
+        put.wait()
 
 
 def collect_kernel(*refs):
@@ -657,8 +674,8 @@
     results = pl.pallas_call(
         backward_kernel,
         out_shape=outs,
-        in_specs=[pl.BlockSpec(memory_space=pltpu.SMEM), ANY, ANY, ANY, ANY, ANY, VM, ANY, ANY],
-        out_specs=(ANY, VM, VM, VM),
+        in_specs=[pl.BlockSpec(memory_space=pltpu.SMEM)] + [ANY] * 8,
+        out_specs=(ANY,) * 4,
         scratch_shapes=[
             vm((T, 2 * HD)), vm((T, 2 * HD)), vm((T, 2 * HD)), vm((T, HD)), vm((T, 2 * HD)),
             vm((HD, T)), vm((HD + 16, T)), vm((T, BF), F32), vm((T, T)), vm((T, T)),
@@ -668,8 +685,9 @@
             vm((D, D)), vm((D, 3 * D)),
             vm((2 * BF, D)), vm((2 * BF, D)), vm((2 * BF, CW)), vm((D, 2 * BF)), vm((D, 2 * BF)),
             vm((2, 4, 2, 4, 16, CW)),
-            vm((2, 16, D), F32), vm((3, 4, 16, D), F32), *buffers,
-            dma((8, NC)), dma((8, NC)), dma((2,)), dma((2,)), dma((5,)), dma((8,)), dma((8,)),
+            vm((2, 16, D), F32), vm((3, 4, 16, D), F32),
+            vm((KW, D), F32), vm((8, 3 * D), F32), vm((8, D), F32), vm((KW, D), F32), *buffers,
+            dma((8, NC)), dma((8, NC)), dma((2,)), dma((2,)), dma((9,)), dma((8,)), dma((8,)),
             dma((NR * 6,)), dma((NR * 6,)), dma((NP * 6,)), dma((NP * 6,)),
             dma((NP * 7,)), dma((NP * 7,)), dma((9,)), dma((9,)),
         ],

time: 102 us -> 92.5 us (0.907)
  Pallas kernels: 101 us -> 91 us
    pallas_call x1, Pallas kernels: 99 us -> 89.1 us  [backward(): pl.pallas_call(backward_kernel, out_shape=outs, in_specs=[pl.BlockSpec(me...]
where the time goes in v4:
time: 92.5 us; the launch traced here: 92.3 us
  Pallas kernels  91 us (98%)
  between operations  1.29 us (1%)
    pallas_call x1, Pallas kernels, backward(): pl.pallas_call(backward_kernel, out_shape=outs, in_specs=[pl.BlockSpec(me...  89.1 us
    pallas_call x1, Pallas kernels, backward(): pl.pallas_call(collect_kernel, out_shape=outs, in_specs=[VM] * 4, out_spe...  1.96 us

profile of v4, /device:TPU:1, one launch (start us, length us, event | category | flops | bytes accessed | tf_op | source)
XLA Modules:
  0.0 92.3 jit_solution(15834030993999226764)
XLA Ops:
  1.3 89.1 %shard_map.120 = (bf16[256,1024]{1,0:T(8,128)(2,1)}, f32[8,3072]{1,0:T(8,128)}, f32[8,1024]{1,0:T(8,128)}, f32[9,1024]{1,0:T(8,128)}) custom-call(s32[1]{0:T(128)S(6)} %copy.13.len_ref, bf16[256,1024]{1,0:T(8,128)(2,1)} %bitcast.6, bf16[256,1024]{1,0:T(8,128)(2,1)} %bitcast.7, bf16[256,1024]{1,0:T(8,128)(2,1)} %bitcast.8, bf16[256,1024]{1,0:T(8,128)(2,1)} %bitcast.9, ...), custom_call_target="tpu_custom_call" | custom-call | tf_op jit(solution)/shard_map/pallas_call | solution.py:674
  90.4 2.0 %shard_map.121 = (bf16[256,1024]{1,0:T(8,128)(2,1)}, f32[8,3072]{1,0:T(8,128)}, f32[8,1024]{1,0:T(8,128)}, f32[9,1024]{1,0:T(8,128)}) custom-call(bf16[256,1024]{1,0:T(8,128)(2,1)} %get-tuple-element.12.refs_0_, f32[8,3072]{1,0:T(8,128)} %get-tuple-element.13.refs_1_, f32[8,1024]{1,0:T(8,128)} %get-tuple-element.14.refs_2_, f32[9,1024]{1,0:T(8,128)} %get-tuple-element.15.refs_3_), custom_call_target="tpu_custom_call" | custom-call | tf_op jit(solution)/shard_map/pallas_call | solution.py:698

commit v5 on v4

--- a/solution.py
+++ b/solution.py
@@ -49,7 +49,6 @@
     (1792, 256, ("z", "y", "x")),
 )
 NP = len(PARTS)
-NR = 6
 
 
 def backward_kernel(
@@ -58,12 +57,12 @@
     q_aug, k_aug, v_aug, do_in, do_aug, k_t, v_t, s_ref, e_ref, ds_ref,
     att_s, linv_s, dq_s, dk_s, dv_s, dat_s, dqkv, din_vm,
     g_vm, gp, dsub, halo_lo, halo_hi, wout_vm, wqkv_vm,
-    li2, att2, r2, li_t, att_t, grads, taps_c, taps_a, conv_vm, dwq_out, dwo_out, dk_out, *rest,
+    li2, att2, r2, li_t, att_t, grads, taps_c, taps_p, taps_a, taps_z, conv_vm, dwq_out, dwo_out, dk_out, *rest,
 ):
-    bufs = rest[: NP * 7]
-    (send_sem, recv_sem, halo_send, halo_recv, local_sem, core_send, core_recv,
+    bufs = rest[: NP * 6]
+    (send_sem, recv_sem, q_recv, halo_send, halo_recv, local_sem, core_send, core_recv,
      ring_send, ring_recv, step_send, step_recv, last_send, last_recv,
-     taps_send, taps_recv) = rest[NP * 7 :]
+     taps_send, taps_recv) = rest[NP * 6 :]
     me = lax.axis_index("ctx")
     rec = lax.axis_index("rec")
     z, y = lax.div(me, 4), lax.rem(me, 4)
@@ -104,13 +103,28 @@
     def remote(t, d):
         p, src, dst = ends(t, d)
         return pltpu.make_async_remote_copy(
-            src_ref=src, dst_ref=dst, send_sem=send_sem.at[t, d], recv_sem=recv_sem.at[t, d],
+            src_ref=src, dst_ref=dst, send_sem=send_sem.at[t],
+            recv_sem=q_recv.at[d] if t == TQ else recv_sem.at[t],
             device_id=(p, rec), device_id_type=MESH,
         )
 
     def local(t):
         _, src, dst = ends(t, 0)
-        return pltpu.make_async_copy(src, dst, recv_sem.at[t, 0])
+        return pltpu.make_async_copy(src, dst, q_recv.at[0] if t == TQ else recv_sem.at[t])
+
+    def whole(ref, sem):
+        pltpu.make_async_copy(ref, ref, sem).wait()
+
+    def drain(sem, count):
+        whole(s_ref.at[pl.ds(0, count // (4 * BF)), :], sem)
+
+    def arrived(t):
+        if t <= TD:
+            whole(fwd_dst[t].at[:, pl.ds(0, HD)], recv_sem.at[t])
+        elif t == BA:
+            whole(att2.at[pl.ds(0, BF), :], recv_sem.at[t])
+        else:
+            whole(dqkv.at[:, pl.ds(back_base[t], D)], recv_sem.at[t])
 
     def each_peer(body):
         def step(d, carry):
@@ -169,11 +183,11 @@
 
     right, left = lax.rem(me + 1, NC), lax.rem(me + NC - 1, NC)
     to_right = pltpu.make_async_remote_copy(
-        src_ref=g_ref.at[pl.ds(BF - 16, 16), :], dst_ref=halo_lo, send_sem=halo_send.at[0],
+        src_ref=g_ref.at[pl.ds(BF - 16, 16), :], dst_ref=halo_lo, send_sem=halo_send,
         recv_sem=halo_recv.at[0], device_id=(right, rec), device_id_type=MESH,
     )
     to_left = pltpu.make_async_remote_copy(
-        src_ref=g_ref.at[pl.ds(0, 16), :], dst_ref=halo_hi, send_sem=halo_send.at[1],
+        src_ref=g_ref.at[pl.ds(0, 16), :], dst_ref=halo_hi, send_sem=halo_send,
         recv_sem=halo_recv.at[1], device_id=(left, rec), device_id_type=MESH,
     )
     to_right.start()
@@ -202,7 +216,7 @@
 
     swap_li = to_partner(4, li_ref, li2.at[theirs, :])
     swap_att = to_partner(5, att2.at[mine, :], att2.at[theirs, :])
-    swap_taps = to_partner(6, taps_c.at[core], taps_c.at[core])
+    swap_taps = to_partner(6, taps_c.at[pl.ds(other * 4, 5)], taps_p)
     swap_li.start()
 
     length = len_ref[0]
@@ -265,10 +279,6 @@
     get_li.wait()
     swap_li.wait_recv()
     turn_in(li2, li_t)
-
-    def arrived(t):
-        local(t).wait()
-        each_peer(lambda d: remote(t, d).wait_recv())
 
     arrived(TK)
     local(TQ).wait()
@@ -312,13 +322,9 @@
     each_slot(attend)
     local(BA).start()
 
-    local(TD).wait()
+    arrived(TD)
 
     def backward_in(d):
-        @pl.when(d > 0)
-        def _():
-            remote(TD, d).wait_recv()
-
         do = (do_in[slot(d), :].astype(F32) * linv_s[d]).astype(BF16)
         delta = -jnp.sum(do.astype(F32) * att_s[d].astype(F32), axis=1, keepdims=True)
         hi = delta.astype(BF16).astype(F32)
@@ -393,9 +399,9 @@
             fixed = {**self.fixed, self.axis: off(self.axis, by)}
             return region(fixed, self.start + start, width)
 
-        def copy(self, sems, n, src, dst, by):
+        def copy(self, src, dst, by, recv):
             return pltpu.make_async_remote_copy(
-                src_ref=src, dst_ref=dst, send_sem=sems[0].at[n], recv_sem=sems[1].at[n],
+                src_ref=src, dst_ref=dst, send_sem=self.send, recv_sem=recv,
                 device_id=device(self.axis, off(self.axis, by)), device_id_type=MESH,
             )
 
@@ -403,31 +409,33 @@
             if self.stage == 0:
                 self.piece(0)[...] = total.astype(BF16)
             else:
-                pair = bufs[self.part * 7 + 5]
+                pair = bufs[self.part * 6 + 4]
                 pair[..., 0, :, :] = total[..., :8, :]
                 pair[..., 1, :, :] = total[..., 8:, :]
 
         def sent(self):
-            for c in self.copies:
-                c.wait_send()
+            drain(self.send, self.sent_bytes)
 
     class Ring(Stage):
         def __init__(self, part):
             super().__init__(part, 0)
-            self.ra, self.rb, self.low, self.high = bufs[part * 7 : part * 7 + 4]
+            self.ra, self.rb, self.ends = bufs[part * 6 : part * 6 + 3]
             h = self.width // 2
-            lead = (slice(None),) * (len(self.low.shape) - 1)
-            a, b = (*lead, pl.ds(0, h)), (*lead, pl.ds(h, h))
-            ends = (
-                (self.piece(2, 0, h), self.ra, 1),
-                (self.piece(2, h, h), self.rb, 3),
-                (self.piece(1, h, h), self.low.at[b], 1),
-                (self.piece(3, 0, h), self.high.at[a], 3),
-                (self.piece(1, 0, h), self.low.at[a], 1),
-                (self.piece(3, h, h), self.high.at[b], 3),
-            )
-            sems = (ring_send, ring_recv)
-            self.copies = [self.copy(sems, part * 6 + n, *e) for n, e in enumerate(ends)]
+            lead = (slice(None),) * (len(self.ra.shape) - 1)
+            low_a, low_b = (0, *lead, pl.ds(0, h)), (0, *lead, pl.ds(h, h))
+            high_a, high_b = (1, *lead, pl.ds(0, h)), (1, *lead, pl.ds(h, h))
+            self.send = ring_send.at[part]
+            self.sent_bytes = 3 * 4 * HALF * self.width // 4 * 2 // 2
+            recv = [ring_recv.at[part * 3 + n] for n in range(3)]
+            self.copies = [
+                self.copy(self.piece(2, 0, h), self.ra, 1, recv[0]),
+                self.copy(self.piece(2, h, h), self.rb, 3, recv[1]),
+                self.copy(self.piece(1, h, h), self.ends.at[low_b], 1, recv[2]),
+                self.copy(self.piece(3, 0, h), self.ends.at[high_a], 3, recv[2]),
+                self.copy(self.piece(1, 0, h), self.ends.at[low_a], 1, recv[2]),
+                self.copy(self.piece(3, h, h), self.ends.at[high_b], 3, recv[2]),
+            ]
+            self.recv = recv[2]
 
         def begin(self):
             for c in self.copies[:4]:
@@ -442,20 +450,18 @@
                 self.copies[4 + n].start()
 
         def end(self):
-            for n in (2, 3, 4, 5):
-                self.copies[n].wait_recv()
+            whole(self.ends, self.recv)
             here = self.piece(0)[...].astype(F32)
-            self.keep(here + (self.low[...].astype(F32) + self.high[...].astype(F32)))
+            self.keep(here + (self.ends[0].astype(F32) + self.ends[1].astype(F32)))
 
     class Direct(Stage):
         def __init__(self, part, stage):
             super().__init__(part, stage)
-            self.buf = bufs[part * 7 + 3 + stage] if stage else bufs[part * 7]
-            base = (part * 2 + stage) * 3
-            sems = (step_send, step_recv)
+            self.buf = bufs[part * 6 + 3]
+            self.send, self.recv = step_send.at[part], step_recv.at[part]
+            self.sent_bytes = 3 * HD // 2 * self.width * 2
             self.copies = [
-                self.copy(sems, base + by - 1, self.piece(by), self.buf.at[by - 1], by)
-                for by in (1, 2, 3)
+                self.copy(self.piece(by), self.buf.at[by - 1], by, self.recv) for by in (1, 2, 3)
             ]
 
         def begin(self):
@@ -463,8 +469,7 @@
                 c.start()
 
         def end(self):
-            for c in self.copies:
-                c.wait_recv()
+            whole(self.buf, self.recv)
             here = self.piece(0)[...].astype(F32)
             b = [self.buf[n].astype(F32) for n in range(3)]
             self.keep((here + b[0]) + (b[1] + b[2]))
@@ -472,7 +477,9 @@
     class Last(Stage):
         def __init__(self, part):
             super().__init__(part, 2)
-            self.pair, self.buf = bufs[part * 7 + 5 : part * 7 + 7]
+            self.pair, self.buf = bufs[part * 6 + 4 : part * 6 + 6]
+            self.send, self.recv = last_send.at[part], last_recv.at[part]
+            self.sent_bytes = 7 * 8 * self.width * 4
             self.copies = []
             for n, (turned, by) in enumerate((t, b) for t in (0, 1) for b in range(4) if t + b):
                 to = lax.rem(core + turned, 2)
@@ -480,7 +487,7 @@
                 self.copies.append(
                     pltpu.make_async_remote_copy(
                         src_ref=self.rows(by, to), dst_ref=self.buf.at[n],
-                        send_sem=last_send.at[part * 7 + n], recv_sem=last_recv.at[part * 7 + n],
+                        send_sem=self.send, recv_sem=self.recv,
                         device_id=who, device_id_type=MESH,
                     )
                 )
@@ -496,8 +503,7 @@
                 c.start()
 
         def end(self):
-            for c in self.copies:
-                c.wait_recv()
+            whole(self.buf, self.recv)
             b = [self.buf[n] for n in range(7)]
             here = self.rows(0, core)[...]
             n, inside = divmod(self.start, HALF)
@@ -509,29 +515,46 @@
                 cols = pl.ds(mult(base + who * HALF + inside, HD), self.width)
                 out[:, cols] = block
 
-    rings = [(Ring(p) if p < NR else Direct(p, 0), Direct(p, 1), Last(p)) for p in range(NP)]
+    rings = [(Ring(p), Direct(p, 1), Last(p)) for p in range(NP)]
 
     def on(p, stage):
         rings[p][stage].end()
         rings[p][stage + 1].begin()
 
-    taps_copies = []
+    def taps_copy(n, src, dst, who):
+        pltpu.make_async_remote_copy(
+            src_ref=src, dst_ref=dst, send_sem=taps_send.at[n], recv_sem=taps_recv.at[n],
+            device_id=who, device_id_type=MESH,
+        ).start()
 
     def taps_on(n, axis, value):
-        taps_a[n, at[axis]] = value
+        here = taps_a.at[n, at[axis]]
+        here[...] = value
         for by in (1, 2, 3):
-            c = pltpu.make_async_remote_copy(
-                src_ref=taps_a.at[n, at[axis]], dst_ref=taps_a.at[n, at[axis]],
-                send_sem=taps_send.at[n * 3 + by - 1], recv_sem=taps_recv.at[n * 3 + by - 1],
-                device_id=device(axis, off(axis, by)), device_id_type=MESH,
-            )
-            c.start()
-            taps_copies.append(c)
+            taps_copy(n, here, here, device(axis, off(axis, by)))
+
+    def taps_last(axis, value):
+        here = taps_z.at[core * 4 + at[axis]]
+        here[...] = value
+        for by in (0, 1, 2, 3):
+            if by:
+                taps_copy(2, here, here, device(axis, off(axis, by)))
+            taps_copy(2, here, here, device(axis, off(axis, by), other))
+
+    def sum_4(ref, n):
+        return (ref[n] + ref[n + 1]) + (ref[n + 2] + ref[n + 3])
 
     def taps_sum(n):
-        for c in taps_copies[n * 3 :]:
-            c.wait_recv()
-        return (taps_a[n, 0] + taps_a[n, 1]) + (taps_a[n, 2] + taps_a[n, 3])
+        whole(taps_a.at[n, pl.ds(0, 3)], taps_recv.at[n])
+        return sum_4(taps_a.at[n], 0)
+
+    def taps_end():
+        whole(taps_z.at[pl.ds(0, 7)], taps_recv.at[2])
+        halves = sum_4(taps_z, 0), sum_4(taps_z, 4)
+        for t in range(KW):
+            block = halves[0][t] if t < 5 else halves[1][t - 4]
+            for n in range(D // HD):
+                dk_out[t : t + 1, n * HD : (n + 1) * HD] = block[n : n + 1, :]
 
     swap_half(OUT).wait_recv()
     swap_att.wait_recv()
@@ -556,9 +579,9 @@
         cols = pl.ds(mult(n * BF, BF), BF)
         sub = dot(att2[mine, :], wout_vm[:, cols]).astype(BF16).astype(F32)
         for t in range(KW):
-            taps_c[core, pl.ds(t, 1), cols] = jnp.sum(
-                sub * gp[pl.ds(12 - t, BF), cols], axis=0, keepdims=True
-            )
+            total = jnp.sum(sub * gp[pl.ds(12 - t, BF), cols], axis=0, keepdims=True)
+            taps_c[t, pl.ds(2 * n, 1), :] = total[:, :HD]
+            taps_c[t, pl.ds(2 * n + 1, 1), :] = total[:, HD:]
 
     def back(t, n):
         arrived(t)
@@ -576,56 +599,55 @@
 
     back(BV, VAL)
     rings[0][0].relay()
-    taps_c[core] = jnp.zeros((16, D), F32)
     lax.fori_loop(0, D // BF, lambda n, c: (taps(n), c)[1], 0)
     swap_taps.start()
     weight(VAL)
+    swap_taps.wait_recv()
+    taps_on(0, "x", taps_c[pl.ds(core * 4, 5)] + taps_p[...])
     rings[1][0].begin()
     back(BQ, QUE)
     get_wq.wait()
-    swap_taps.wait_recv()
-    taps_on(0, "x", taps_c[0] + taps_c[1])
     weight(QUE)
     rings[2][0].begin()
     rings[3][0].begin()
     back(BK, KEY)
+    taps_on(1, "y", taps_sum(0))
     lax.fori_loop(0, 2, d_input, 0)
     weight(KEY)
     rings[4][0].begin()
     rings[5][0].begin()
-    rings[1][0].relay()
     rings[2][0].relay()
     rings[3][0].relay()
-    on(0, 0)
+    rings[1][0].relay()
+    taps_last("z", taps_sum(1))
     rings[4][0].relay()
     rings[5][0].relay()
+    on(0, 0)
     lax.fori_loop(2, 4, d_input, 0)
     put_din = pltpu.make_async_copy(din_vm, din_hbm, local_sem.at[4])
     put_din.start()
-    taps_on(1, "y", taps_sum(0))
     on(2, 0)
     on(3, 0)
-    on(0, 1)
     on(1, 0)
     on(4, 0)
     on(5, 0)
-    taps_on(2, "z", taps_sum(1))
-    for p in (2, 3, 1, 4, 5):
-        on(p, 1)
-    dk_out[...] = taps_sum(2)[:KW]
+    on(0, 1)
+    taps_end()
     puts = [
         pltpu.make_async_copy(a, b, local_sem.at[n])
         for a, b, n in ((dk_out, dk_hbm, 6), (dwo_out, dwo_hbm, 7), (dwq_out, dwq_hbm, 8))
     ]
     puts[0].start()
-    to_right.wait_send()
-    to_left.wait_send()
+    for p in (2, 3, 1, 4, 5):
+        on(p, 1)
+    whole(att2.at[pl.ds(0, 32), :], halo_send)
     for t in range(8):
-        each_peer(lambda d: remote(t, d).wait_send())
+        drain(send_sem.at[t], (NC - 1) * BF * HD * 2)
     for swap in (swap_li, swap_att, swap_taps, *(swap_half(n) for n in range(4))):
         swap.wait_send()
-    for c in taps_copies:
-        c.wait_send()
+    for n in (0, 1):
+        whole(taps_a.at[n, pl.ds(0, 3)], taps_send.at[n])
+    whole(taps_z.at[pl.ds(0, 7)], taps_send.at[2])
     for r in rings:
         r[0].sent()
         r[1].sent()
@@ -651,16 +673,13 @@
         return pltpu.VMEM(shape, dtype)
 
     buffers = []
-    for p, (_, width, order) in enumerate(PARTS):
+    for _, width, order in PARTS:
         leads = []
         for stage in range(3):
             sizes = (("zl", 2), ("y", 4), ("zh", 2), ("x", 4))
             leads.append([n for axis, n in sizes if axis[0] not in order[: stage + 1]])
-        if p < NR:
-            first = [(*leads[0], 16, w) for w in (width // 2, width // 2, width, width)]
-        else:
-            first = [(3, *leads[0], 16, width)] + [(16, HD)] * 3
-        buffers += [vm(shape) for shape in first]
+        halves = [(*leads[0], 16, width // 2)] * 2
+        buffers += [vm(shape) for shape in (*halves, (2, *leads[0], 16, width))]
         buffers.append(vm((3, *leads[1], 16, width)))
         buffers.append(vm((*leads[1], 2, 8, width), F32))
         buffers.append(vm((7, 8, width), F32))
@@ -685,11 +704,11 @@
             vm((D, D)), vm((D, 3 * D)),
             vm((2 * BF, D)), vm((2 * BF, D)), vm((2 * BF, CW)), vm((D, 2 * BF)), vm((D, 2 * BF)),
             vm((2, 4, 2, 4, 16, CW)),
-            vm((2, 16, D), F32), vm((3, 4, 16, D), F32),
+            vm((KW, 8, HD), F32), vm((5, 8, HD), F32), vm((2, 4, 5, 8, HD), F32), vm((8, 5, 8, HD), F32),
             vm((KW, D), F32), vm((8, 3 * D), F32), vm((8, D), F32), vm((KW, D), F32), *buffers,
-            dma((8, NC)), dma((8, NC)), dma((2,)), dma((2,)), dma((9,)), dma((8,)), dma((8,)),
-            dma((NR * 6,)), dma((NR * 6,)), dma((NP * 6,)), dma((NP * 6,)),
-            dma((NP * 7,)), dma((NP * 7,)), dma((9,)), dma((9,)),
+            dma((8,)), dma((8,)), dma((NC,)), dma(()), dma((2,)), dma((9,)), dma((7,)), dma((7,)),
+            dma((NP,)), dma((NP * 3,)), dma((NP,)), dma((NP,)), dma((NP,)), dma((NP,)),
+            dma((3,)), dma((3,)),
         ],
         compiler_params=pltpu.CompilerParams(
             collective_id=0, has_side_effects=True, vmem_limit_bytes=60 * 1024 * 1024

time: 92.5 us -> 87.5 us (0.946)
  Pallas kernels: 91 us -> 85.9 us
    pallas_call x1, Pallas kernels: 89.1 us -> 84 us  [backward(): pl.pallas_call(backward_kernel, out_shape=outs, in_specs=[pl.BlockSpec(me...]
where the time goes in v5:
time: 87.5 us; the launch traced here: 87.2 us
  Pallas kernels  85.9 us (98%)
  between operations  1.29 us (1%)
    pallas_call x1, Pallas kernels, backward(): pl.pallas_call(backward_kernel, out_shape=outs, in_specs=[pl.BlockSpec(me...  84 us
    pallas_call x1, Pallas kernels, backward(): pl.pallas_call(collect_kernel, out_shape=outs, in_specs=[VM] * 4, out_spe...  1.96 us

profile of v5, /device:TPU:1, one launch (start us, length us, event | category | flops | bytes accessed | tf_op | source)
XLA Modules:
  0.0 87.2 jit_solution(16937837303258992884)
XLA Ops:
  1.3 84.0 %shard_map.120 = (bf16[256,1024]{1,0:T(8,128)(2,1)}, f32[8,3072]{1,0:T(8,128)}, f32[8,1024]{1,0:T(8,128)}, f32[9,1024]{1,0:T(8,128)}) custom-call(s32[1]{0:T(128)S(6)} %copy.13.len_ref, bf16[256,1024]{1,0:T(8,128)(2,1)} %bitcast.6, bf16[256,1024]{1,0:T(8,128)(2,1)} %bitcast.7, bf16[256,1024]{1,0:T(8,128)(2,1)} %bitcast.8, bf16[256,1024]{1,0:T(8,128)(2,1)} %bitcast.9, ...), custom_call_target="tpu_custom_call" | custom-call | tf_op jit(solution)/shard_map/pallas_call | solution.py:693
  85.3 2.0 %shard_map.121 = (bf16[256,1024]{1,0:T(8,128)(2,1)}, f32[8,3072]{1,0:T(8,128)}, f32[8,1024]{1,0:T(8,128)}, f32[9,1024]{1,0:T(8,128)}) custom-call(bf16[256,1024]{1,0:T(8,128)(2,1)} %get-tuple-element.12.refs_0_, f32[8,3072]{1,0:T(8,128)} %get-tuple-element.13.refs_1_, f32[8,1024]{1,0:T(8,128)} %get-tuple-element.14.refs_2_, f32[9,1024]{1,0:T(8,128)} %get-tuple-element.15.refs_3_), custom_call_target="tpu_custom_call" | custom-call | tf_op jit(solution)/shard_map/pallas_call | solution.py:717

commit v6 on v5

--- a/solution.py
+++ b/solution.py
@@ -45,19 +45,21 @@
     (512, 512, ("x", "z", "y")),
     (1024, 256, ("y", "x", "z")),
     (1280, 256, ("z", "x", "y")),
-    (1536, 256, ("y", "z", "x")),
-    (1792, 256, ("z", "y", "x")),
+    (1536, 256, ("x", "y", "z")),
+    (1792, 128, ("y", "z", "x")),
+    (1920, 128, ("z", "y", "x")),
 )
+RINGS = (0, 1, 2, 3)
 NP = len(PARTS)
 
 
 def backward_kernel(
     len_ref, li_ref, q_ref, k_ref, v_ref, g_ref, conv_ref, wout_ref, wqkv_ref,
-    din_hbm, dwq_hbm, dwo_hbm, dk_hbm,
+    din_vm, dwq_out, dwo_out, dk_out,
     q_aug, k_aug, v_aug, do_in, do_aug, k_t, v_t, s_ref, e_ref, ds_ref,
-    att_s, linv_s, dq_s, dk_s, dv_s, dat_s, dqkv, din_vm,
+    att_s, linv_s, dq_s, dk_s, dv_s, dat_s, dqkv,
     g_vm, gp, dsub, halo_lo, halo_hi, wout_vm, wqkv_vm,
-    li2, att2, r2, li_t, att_t, grads, taps_c, taps_p, taps_a, taps_z, conv_vm, dwq_out, dwo_out, dk_out, *rest,
+    li2, att2, r2, li_t, att_t, grads, taps_c, taps_p, taps_a, taps_z, conv_vm, *rest,
 ):
     bufs = rest[: NP * 6]
     (send_sem, recv_sem, q_recv, halo_send, halo_recv, local_sem, core_send, core_recv,
@@ -363,12 +365,6 @@
         def _():
             remote(BQ, d).start()
 
-    lax.fori_loop(0, 5, lambda d, c: (d_query(d), c)[1], 0)
-    arrived(BA)
-    swap_att.start()
-    lax.fori_loop(5, NC, lambda d, c: (d_query(d), c)[1], 0)
-    local(BQ).start()
-
     def product(lhs, start, width):
         def step(zl, carry):
             rows = pl.ds(mult(zl * HALF, HALF), HALF)
@@ -410,11 +406,15 @@
                 self.piece(0)[...] = total.astype(BF16)
             else:
                 pair = bufs[self.part * 6 + 4]
-                pair[..., 0, :, :] = total[..., :8, :]
-                pair[..., 1, :, :] = total[..., 8:, :]
+                for c in (0, 1):
+                    rows = total[..., c * 8 : c * 8 + 8, :]
+                    if self.width > HD:
+                        h = self.width // 2
+                        rows = jnp.concatenate([rows[..., :h], rows[..., h:]], axis=-2)
+                    pair[..., c, :, :] = rows.astype(pair.dtype)
 
         def sent(self):
-            drain(self.send, self.sent_bytes)
+            whole(self.buf, self.send)
 
     class Ring(Stage):
         def __init__(self, part):
@@ -425,7 +425,6 @@
             low_a, low_b = (0, *lead, pl.ds(0, h)), (0, *lead, pl.ds(h, h))
             high_a, high_b = (1, *lead, pl.ds(0, h)), (1, *lead, pl.ds(h, h))
             self.send = ring_send.at[part]
-            self.sent_bytes = 3 * 4 * HALF * self.width // 4 * 2 // 2
             recv = [ring_recv.at[part * 3 + n] for n in range(3)]
             self.copies = [
                 self.copy(self.piece(2, 0, h), self.ra, 1, recv[0]),
@@ -441,6 +440,9 @@
             for c in self.copies[:4]:
                 c.start()
 
+        def sent(self):
+            drain(self.send, 3 * BF * self.width * 2)
+
         def relay(self):
             h = self.width // 2
             for n, by, buf, start in ((0, 1, self.ra, 0), (1, 3, self.rb, h)):
@@ -457,9 +459,9 @@
     class Direct(Stage):
         def __init__(self, part, stage):
             super().__init__(part, stage)
-            self.buf = bufs[part * 6 + 3]
-            self.send, self.recv = step_send.at[part], step_recv.at[part]
-            self.sent_bytes = 3 * HD // 2 * self.width * 2
+            self.buf = bufs[part * 6 + (3 if stage else 2)]
+            n = part if stage else NP + part
+            self.send, self.recv = step_send.at[n], step_recv.at[n]
             self.copies = [
                 self.copy(self.piece(by), self.buf.at[by - 1], by, self.recv) for by in (1, 2, 3)
             ]
@@ -479,7 +481,6 @@
             super().__init__(part, 2)
             self.pair, self.buf = bufs[part * 6 + 4 : part * 6 + 6]
             self.send, self.recv = last_send.at[part], last_recv.at[part]
-            self.sent_bytes = 7 * 8 * self.width * 4
             self.copies = []
             for n, (turned, by) in enumerate((t, b) for t in (0, 1) for b in range(4) if t + b):
                 to = lax.rem(core + turned, 2)
@@ -504,18 +505,25 @@
 
         def end(self):
             whole(self.buf, self.recv)
-            b = [self.buf[n] for n in range(7)]
-            here = self.rows(0, core)[...]
+            b = [self.buf[n].astype(F32) for n in range(7)]
+            here = self.rows(0, core)[...].astype(F32)
             n, inside = divmod(self.start, HALF)
             out, base = ((dwo_out, 0), (dwq_out, 2 * D), (dwq_out, 0), (dwq_out, D))[n]
             for who, block in (
                 (core, (here + b[0]) + (b[1] + b[2])),
                 (other, (b[3] + b[4]) + (b[5] + b[6])),
             ):
-                cols = pl.ds(mult(base + who * HALF + inside, HD), self.width)
-                out[:, cols] = block
-
-    rings = [(Ring(p), Direct(p, 1), Last(p)) for p in range(NP)]
+                first = base + who * HALF + inside
+                if self.width > HD:
+                    h = self.width // 2
+                    out[:, pl.ds(mult(first, HD), h)] = block[:8]
+                    out[:, pl.ds(mult(first + h, HD), h)] = block[8:]
+                else:
+                    out[:, pl.ds(mult(first, HD), HD)] = block
+
+    rings = [
+        (Ring(p) if p in RINGS else Direct(p, 0), Direct(p, 1), Last(p)) for p in range(NP)
+    ]
 
     def on(p, stage):
         rings[p][stage].end()
@@ -556,25 +564,6 @@
             for n in range(D // HD):
                 dk_out[t : t + 1, n * HD : (n + 1) * HD] = block[n : n + 1, :]
 
-    swap_half(OUT).wait_recv()
-    swap_att.wait_recv()
-    turn_in(att2, att_t)
-    product(att_t, OUT * HALF, HALF)
-    rings[0][0].begin()
-
-    def d_key(j):
-        two = pl.ds(mult(j * 2 * BF, 2 * BF), 2 * BF)
-        dk_s[pl.ds(j * 2, 2)] = (dot(ds_ref[two, :], q_aug[:, pl.ds(0, HD)]) * inv_root).astype(BF16).reshape(2, BF, HD)
-
-        @pl.when(j > 0)
-        def _():
-            remote(BK, j * 2).start()
-
-        remote(BK, j * 2 + 1).start()
-
-    lax.fori_loop(0, NC // 2, lambda j, c: (d_key(j), c)[1], 0)
-    local(BK).start()
-
     def taps(n):
         cols = pl.ds(mult(n * BF, BF), BF)
         sub = dot(att2[mine, :], wout_vm[:, cols]).astype(BF16).astype(F32)
@@ -597,49 +586,66 @@
         din_vm[:, cols] = dot_nt(dqkv[...], wqkv_vm[cols, :]).astype(BF16)
         return carry
 
+    lax.fori_loop(0, 3, lambda d, c: (d_query(d), c)[1], 0)
+    arrived(BA)
+    swap_att.start()
+    lax.fori_loop(3, 5, lambda d, c: (d_query(d), c)[1], 0)
+
+    swap_half(OUT).wait_recv()
+    swap_att.wait_recv()
+    turn_in(att2, att_t)
+    product(att_t, OUT * HALF, HALF)
+    rings[0][0].begin()
+    lax.fori_loop(0, D // BF, lambda n, c: (taps(n), c)[1], 0)
+    swap_taps.start()
+    lax.fori_loop(5, NC, lambda d, c: (d_query(d), c)[1], 0)
+    local(BQ).start()
     back(BV, VAL)
     rings[0][0].relay()
-    lax.fori_loop(0, D // BF, lambda n, c: (taps(n), c)[1], 0)
-    swap_taps.start()
-    weight(VAL)
     swap_taps.wait_recv()
     taps_on(0, "x", taps_c[pl.ds(core * 4, 5)] + taps_p[...])
+
+    def d_key(j):
+        two = pl.ds(mult(j * 2 * BF, 2 * BF), 2 * BF)
+        dk_s[pl.ds(j * 2, 2)] = (dot(ds_ref[two, :], q_aug[:, pl.ds(0, HD)]) * inv_root).astype(BF16).reshape(2, BF, HD)
+
+        @pl.when(j > 0)
+        def _():
+            remote(BK, j * 2).start()
+
+        remote(BK, j * 2 + 1).start()
+
+    lax.fori_loop(0, 2, lambda j, c: (d_key(j), c)[1], 0)
+    weight(VAL)
     rings[1][0].begin()
+    lax.fori_loop(2, NC // 2, lambda j, c: (d_key(j), c)[1], 0)
+    local(BK).start()
     back(BQ, QUE)
     get_wq.wait()
     weight(QUE)
     rings[2][0].begin()
     rings[3][0].begin()
+    rings[1][0].relay()
+    taps_on(1, "y", taps_sum(0))
     back(BK, KEY)
-    taps_on(1, "y", taps_sum(0))
     lax.fori_loop(0, 2, d_input, 0)
     weight(KEY)
-    rings[4][0].begin()
-    rings[5][0].begin()
+    for p in (5, 6, 4):
+        rings[p][0].begin()
     rings[2][0].relay()
     rings[3][0].relay()
-    rings[1][0].relay()
     taps_last("z", taps_sum(1))
-    rings[4][0].relay()
-    rings[5][0].relay()
     on(0, 0)
     lax.fori_loop(2, 4, d_input, 0)
-    put_din = pltpu.make_async_copy(din_vm, din_hbm, local_sem.at[4])
-    put_din.start()
+    on(1, 0)
+    on(5, 0)
+    on(6, 0)
     on(2, 0)
     on(3, 0)
-    on(1, 0)
     on(4, 0)
-    on(5, 0)
-    on(0, 1)
+    for p in (0, 1, 5, 6, 2, 3, 4):
+        on(p, 1)
     taps_end()
-    puts = [
-        pltpu.make_async_copy(a, b, local_sem.at[n])
-        for a, b, n in ((dk_out, dk_hbm, 6), (dwo_out, dwo_hbm, 7), (dwq_out, dwq_hbm, 8))
-    ]
-    puts[0].start()
-    for p in (2, 3, 1, 4, 5):
-        on(p, 1)
     whole(att2.at[pl.ds(0, 32), :], halo_send)
     for t in range(8):
         drain(send_sem.at[t], (NC - 1) * BF * HD * 2)
@@ -651,21 +657,19 @@
     for r in rings:
         r[0].sent()
         r[1].sent()
-    rings[0][2].end()
-    puts[1].start()
-    for p in range(1, NP):
+    for p in (0, 1, 5, 6, 2, 3, 4):
         rings[p][2].end()
-    puts[2].start()
     for r in rings:
         r[2].sent()
-    put_din.wait()
-    for put in puts:
-        put.wait()
 
 
 def collect_kernel(*refs):
-    for a, b in zip(refs[:4], refs[4:]):
-        b[...] = a[...]
+    ins, outs, sems = refs[:4], refs[4:8], refs[8]
+    copies = [pltpu.make_async_copy(a, b, sems.at[n]) for n, (a, b) in enumerate(zip(ins, outs))]
+    for c in copies:
+        c.start()
+    for c in copies:
+        c.wait()
 
 
 def backward(lengths, li, q, k, v, g, conv, wout, wqkv):
@@ -673,16 +677,18 @@
         return pltpu.VMEM(shape, dtype)
 
     buffers = []
-    for _, width, order in PARTS:
+    for p, (_, width, order) in enumerate(PARTS):
         leads = []
         for stage in range(3):
             sizes = (("zl", 2), ("y", 4), ("zh", 2), ("x", 4))
             leads.append([n for axis, n in sizes if axis[0] not in order[: stage + 1]])
         halves = [(*leads[0], 16, width // 2)] * 2
-        buffers += [vm(shape) for shape in (*halves, (2, *leads[0], 16, width))]
+        sides = 2 if p in RINGS else 3
+        buffers += [vm(shape) for shape in (*halves, (sides, *leads[0], 16, width))]
         buffers.append(vm((3, *leads[1], 16, width)))
-        buffers.append(vm((*leads[1], 2, 8, width), F32))
-        buffers.append(vm((7, 8, width), F32))
+        block, kind = ((16, width // 2), BF16) if width > HD else ((8, width), F32)
+        buffers.append(vm((*leads[1], 2, *block), kind))
+        buffers.append(vm((7, *block), kind))
     dma = pltpu.SemaphoreType.DMA
     outs = (
         jax.ShapeDtypeStruct((BF, D), BF16),
@@ -692,33 +698,35 @@
     )
     results = pl.pallas_call(
         backward_kernel,
-        out_shape=outs,
+        out_shape=tuple(pltpu.VMEM(o.shape, o.dtype) for o in outs),
         in_specs=[pl.BlockSpec(memory_space=pltpu.SMEM)] + [ANY] * 8,
-        out_specs=(ANY,) * 4,
+        out_specs=(VM,) * 4,
         scratch_shapes=[
             vm((T, 2 * HD)), vm((T, 2 * HD)), vm((T, 2 * HD)), vm((T, HD)), vm((T, 2 * HD)),
             vm((HD, T)), vm((HD + 16, T)), vm((T, BF), F32), vm((T, T)), vm((T, T)),
             vm((NC, BF, HD)), vm((NC, BF, HD), F32), vm((NC, BF, HD)), vm((NC, BF, HD)),
-            vm((NC, BF, HD)), vm((NC, BF, HD)), vm((BF, 3 * D)), vm((BF, D)),
+            vm((NC, BF, HD)), vm((NC, BF, HD)), vm((BF, 3 * D)),
             vm((BF, D)), vm((BF + 16, D), F32), vm((BF, D)), vm((16, D)), vm((16, D)),
             vm((D, D)), vm((D, 3 * D)),
             vm((2 * BF, D)), vm((2 * BF, D)), vm((2 * BF, CW)), vm((D, 2 * BF)), vm((D, 2 * BF)),
             vm((2, 4, 2, 4, 16, CW)),
             vm((KW, 8, HD), F32), vm((5, 8, HD), F32), vm((2, 4, 5, 8, HD), F32), vm((8, 5, 8, HD), F32),
-            vm((KW, D), F32), vm((8, 3 * D), F32), vm((8, D), F32), vm((KW, D), F32), *buffers,
-            dma((8,)), dma((8,)), dma((NC,)), dma(()), dma((2,)), dma((9,)), dma((7,)), dma((7,)),
-            dma((NP,)), dma((NP * 3,)), dma((NP,)), dma((NP,)), dma((NP,)), dma((NP,)),
+            vm((KW, D), F32), *buffers,
+            dma((8,)), dma((8,)), dma((NC,)), dma(()), dma((2,)), dma((6,)), dma((7,)), dma((7,)),
+            dma((NP,)), dma((NP * 3,)), dma((2 * NP,)), dma((2 * NP,)), dma((NP,)), dma((NP,)),
             dma((3,)), dma((3,)),
         ],
         compiler_params=pltpu.CompilerParams(
             collective_id=0, has_side_effects=True, vmem_limit_bytes=60 * 1024 * 1024
         ),
     )(lengths, li, q, k, v, g, conv, wout, wqkv)
+    results = [pltpu.with_memory_space_constraint(r, pltpu.VMEM) for r in results]
     return pl.pallas_call(
         collect_kernel,
         out_shape=outs,
         in_specs=[VM] * 4,
-        out_specs=(VM,) * 4,
+        out_specs=(ANY,) * 4,
+        scratch_shapes=[dma((4,))],
     )(*results)
 
 

time: 87.5 us -> 84 us (0.960)
  Pallas kernels: 85.9 us -> 82.6 us
    pallas_call x1, Pallas kernels: 84 us -> 81.7 us  [backward(): pl.pallas_call(backward_kernel, out_shape=tuple((pltpu.VMEM(o.shape, o.dt...]
    pallas_call x1, Pallas kernels: 1.96 us -> 0.88 us  [backward(): pl.pallas_call(collect_kernel, out_shape=outs, in_specs=[VM] * 4, out_spe...]
where the time goes in v6:
time: 84 us; the launch traced here: 83.9 us
  Pallas kernels  82.6 us (98%)
  between operations  1.29 us (2%)
    pallas_call x1, Pallas kernels, backward(): pl.pallas_call(backward_kernel, out_shape=tuple((pltpu.VMEM(o.shape, o.dt...  81.7 us

profile of v6, /device:TPU:1, one launch (start us, length us, event | category | flops | bytes accessed | tf_op | source)
XLA Modules:
  0.0 83.9 jit_solution(4667268662799379301)
XLA Ops:
  1.3 81.7 %shard_map.120 = (bf16[256,1024]{1,0:T(8,128)(2,1)S(1)}, f32[8,3072]{1,0:T(8,128)S(1)}, f32[8,1024]{1,0:T(8,128)S(1)}, f32[9,1024]{1,0:T(8,128)S(1)}) custom-call(s32[1]{0:T(128)S(6)} %copy.13.len_ref, bf16[256,1024]{1,0:T(8,128)(2,1)} %bitcast.6, bf16[256,1024]{1,0:T(8,128)(2,1)} %bitcast.7, bf16[256,1024]{1,0:T(8,128)(2,1)} %bitcast.8, ...), custom_call_target="tpu_custom_call" | custom-call | tf_op jit(solution)/shard_map/pallas_call | solution.py:699
  83.0 0.9 %shard_map.121 = (bf16[256,1024]{1,0:T(8,128)(2,1)}, f32[8,3072]{1,0:T(8,128)}, f32[8,1024]{1,0:T(8,128)}, f32[9,1024]{1,0:T(8,128)}) custom-call(bf16[256,1024]{1,0:T(8,128)(2,1)S(1)} %get-tuple-element.12.refs_0_, f32[8,3072]{1,0:T(8,128)S(1)} %get-tuple-element.13.refs_1_, f32[8,1024]{1,0:T(8,128)S(1)} %get-tuple-element.14.refs_2_, ...), custom_call_target="tpu_custom_call" | custom-call | tf_op jit(solution)/shard_map/pallas_call | solution.py:724

commit v7 on v6

--- a/solution.py
+++ b/solution.py
@@ -45,21 +45,21 @@
     (512, 512, ("x", "z", "y")),
     (1024, 256, ("y", "x", "z")),
     (1280, 256, ("z", "x", "y")),
-    (1536, 256, ("x", "y", "z")),
-    (1792, 128, ("y", "z", "x")),
-    (1920, 128, ("z", "y", "x")),
+    (1536, 128, ("x", "y", "z")),
+    (1664, 128, ("y", "x", "z")),
+    (1792, 256, ("z", "y", "x")),
 )
 RINGS = (0, 1, 2, 3)
 NP = len(PARTS)
 
 
 def backward_kernel(
-    len_ref, li_ref, q_ref, k_ref, v_ref, g_ref, conv_ref, wout_ref, wqkv_ref,
+    len_hbm, li_ref, q_ref, k_ref, v_ref, g_ref, conv_ref, wout_ref, wqkv_ref,
     din_vm, dwq_out, dwo_out, dk_out,
     q_aug, k_aug, v_aug, do_in, do_aug, k_t, v_t, s_ref, e_ref, ds_ref,
     att_s, linv_s, dq_s, dk_s, dv_s, dat_s, dqkv,
     g_vm, gp, dsub, halo_lo, halo_hi, wout_vm, wqkv_vm,
-    li2, att2, r2, li_t, att_t, grads, taps_c, taps_p, taps_a, taps_z, conv_vm, *rest,
+    li2, att2, r2, li_t, att_t, grads, taps_c, taps_p, taps_a, taps_z, conv_vm, len_ref, *rest,
 ):
     bufs = rest[: NP * 6]
     (send_sem, recv_sem, q_recv, halo_send, halo_recv, local_sem, core_send, core_recv,
@@ -105,7 +105,7 @@
     def remote(t, d):
         p, src, dst = ends(t, d)
         return pltpu.make_async_remote_copy(
-            src_ref=src, dst_ref=dst, send_sem=send_sem.at[t],
+            src_ref=src, dst_ref=dst, send_sem=send_sem,
             recv_sem=q_recv.at[d] if t == TQ else recv_sem.at[t],
             device_id=(p, rec), device_id_type=MESH,
         )
@@ -118,7 +118,7 @@
         pltpu.make_async_copy(ref, ref, sem).wait()
 
     def drain(sem, count):
-        whole(s_ref.at[pl.ds(0, count // (4 * BF)), :], sem)
+        whole(e_ref.at[pl.ds(0, count // (2 * T)), :], sem)
 
     def arrived(t):
         if t <= TD:
@@ -154,6 +154,8 @@
     get_wq = pltpu.make_async_copy(wqkv_ref, wqkv_vm, local_sem.at[3])
     get_conv = pltpu.make_async_copy(conv_ref, conv_vm, local_sem.at[5])
     get_conv.start()
+    get_len = pltpu.make_async_copy(len_hbm, len_ref, local_sem.at[4])
+    get_len.start()
 
     core = lax.rem(rec, 2)
     other = 1 - core
@@ -199,7 +201,7 @@
 
     def to_partner(n, src, dst):
         return pltpu.make_async_remote_copy(
-            src_ref=src, dst_ref=dst, send_sem=core_send.at[n], recv_sem=core_recv.at[n],
+            src_ref=src, dst_ref=dst, send_sem=core_send.at[n // 6], recv_sem=core_recv.at[n],
             device_id=partner, device_id_type=MESH,
         )
 
@@ -221,6 +223,7 @@
     swap_taps = to_partner(6, taps_c.at[pl.ds(other * 4, 5)], taps_p)
     swap_li.start()
 
+    get_len.wait()
     length = len_ref[0]
     lane = lax.broadcasted_iota(jnp.int32, (BF, HD), 1)
     row = lax.broadcasted_iota(jnp.int32, (BF, HD), 0)
@@ -413,9 +416,6 @@
                         rows = jnp.concatenate([rows[..., :h], rows[..., h:]], axis=-2)
                     pair[..., c, :, :] = rows.astype(pair.dtype)
 
-        def sent(self):
-            whole(self.buf, self.send)
-
     class Ring(Stage):
         def __init__(self, part):
             super().__init__(part, 0)
@@ -424,7 +424,7 @@
             lead = (slice(None),) * (len(self.ra.shape) - 1)
             low_a, low_b = (0, *lead, pl.ds(0, h)), (0, *lead, pl.ds(h, h))
             high_a, high_b = (1, *lead, pl.ds(0, h)), (1, *lead, pl.ds(h, h))
-            self.send = ring_send.at[part]
+            self.send = ring_send
             recv = [ring_recv.at[part * 3 + n] for n in range(3)]
             self.copies = [
                 self.copy(self.piece(2, 0, h), self.ra, 1, recv[0]),
@@ -440,9 +440,6 @@
             for c in self.copies[:4]:
                 c.start()
 
-        def sent(self):
-            drain(self.send, 3 * BF * self.width * 2)
-
         def relay(self):
             h = self.width // 2
             for n, by, buf, start in ((0, 1, self.ra, 0), (1, 3, self.rb, h)):
@@ -461,7 +458,7 @@
             super().__init__(part, stage)
             self.buf = bufs[part * 6 + (3 if stage else 2)]
             n = part if stage else NP + part
-            self.send, self.recv = step_send.at[n], step_recv.at[n]
+            self.send, self.recv = step_send.at[min(stage, 1)], step_recv.at[n]
             self.copies = [
                 self.copy(self.piece(by), self.buf.at[by - 1], by, self.recv) for by in (1, 2, 3)
             ]
@@ -480,7 +477,7 @@
         def __init__(self, part):
             super().__init__(part, 2)
             self.pair, self.buf = bufs[part * 6 + 4 : part * 6 + 6]
-            self.send, self.recv = last_send.at[part], last_recv.at[part]
+            self.send, self.recv = last_send, last_recv.at[part]
             self.copies = []
             for n, (turned, by) in enumerate((t, b) for t in (0, 1) for b in range(4) if t + b):
                 to = lax.rem(core + turned, 2)
@@ -596,14 +593,8 @@
     turn_in(att2, att_t)
     product(att_t, OUT * HALF, HALF)
     rings[0][0].begin()
-    lax.fori_loop(0, D // BF, lambda n, c: (taps(n), c)[1], 0)
-    swap_taps.start()
     lax.fori_loop(5, NC, lambda d, c: (d_query(d), c)[1], 0)
     local(BQ).start()
-    back(BV, VAL)
-    rings[0][0].relay()
-    swap_taps.wait_recv()
-    taps_on(0, "x", taps_c[pl.ds(core * 4, 5)] + taps_p[...])
 
     def d_key(j):
         two = pl.ds(mult(j * 2 * BF, 2 * BF), 2 * BF)
@@ -616,51 +607,61 @@
         remote(BK, j * 2 + 1).start()
 
     lax.fori_loop(0, 2, lambda j, c: (d_key(j), c)[1], 0)
+    back(BV, VAL)
+    rings[0][0].relay()
     weight(VAL)
     rings[1][0].begin()
     lax.fori_loop(2, NC // 2, lambda j, c: (d_key(j), c)[1], 0)
     local(BK).start()
     back(BQ, QUE)
-    get_wq.wait()
+    lax.fori_loop(0, D // BF, lambda n, c: (taps(n), c)[1], 0)
+    swap_taps.start()
     weight(QUE)
     rings[2][0].begin()
     rings[3][0].begin()
-    rings[1][0].relay()
-    taps_on(1, "y", taps_sum(0))
+    swap_taps.wait_recv()
+    taps_on(0, "x", taps_c[pl.ds(core * 4, 5)] + taps_p[...])
+    get_wq.wait()
     back(BK, KEY)
     lax.fori_loop(0, 2, d_input, 0)
+    rings[1][0].relay()
+    rings[2][0].relay()
+    rings[3][0].relay()
     weight(KEY)
     for p in (5, 6, 4):
         rings[p][0].begin()
-    rings[2][0].relay()
-    rings[3][0].relay()
-    taps_last("z", taps_sum(1))
     on(0, 0)
     lax.fori_loop(2, 4, d_input, 0)
     on(1, 0)
-    on(5, 0)
-    on(6, 0)
+    taps_on(1, "y", taps_sum(0))
     on(2, 0)
     on(3, 0)
+    on(5, 0)
     on(4, 0)
-    for p in (0, 1, 5, 6, 2, 3, 4):
-        on(p, 1)
-    taps_end()
+    on(6, 0)
+    on(0, 1)
+    on(2, 1)
+    on(3, 1)
+    on(5, 1)
+    on(1, 1)
+    taps_last("z", taps_sum(1))
+    on(4, 1)
+    on(6, 1)
     whole(att2.at[pl.ds(0, 32), :], halo_send)
-    for t in range(8):
-        drain(send_sem.at[t], (NC - 1) * BF * HD * 2)
-    for swap in (swap_li, swap_att, swap_taps, *(swap_half(n) for n in range(4))):
-        swap.wait_send()
+    drain(send_sem, 8 * (NC - 1) * BF * HD * 2)
+    drain(core_send.at[0], 4 * BF * D * 2)
+    swap_taps.wait_send()
     for n in (0, 1):
         whole(taps_a.at[n, pl.ds(0, 3)], taps_send.at[n])
     whole(taps_z.at[pl.ds(0, 7)], taps_send.at[2])
-    for r in rings:
-        r[0].sent()
-        r[1].sent()
-    for p in (0, 1, 5, 6, 2, 3, 4):
+    ring_width = sum(PARTS[p][1] for p in RINGS)
+    drain(ring_send, 3 * BF * ring_width * 2)
+    drain(step_send.at[0], 3 * BF * (CW - ring_width) * 2)
+    drain(step_send.at[1], 3 * BF // 4 * CW * 2)
+    for p in (0, 2, 3, 5, 1, 4, 6):
         rings[p][2].end()
-    for r in rings:
-        r[2].sent()
+    taps_end()
+    whole(do_in.at[pl.ds(0, 7 * 8 * (CW + 2 * HD) * 2 // (2 * HD)), :], last_send)
 
 
 def collect_kernel(*refs):
@@ -699,7 +700,7 @@
     results = pl.pallas_call(
         backward_kernel,
         out_shape=tuple(pltpu.VMEM(o.shape, o.dtype) for o in outs),
-        in_specs=[pl.BlockSpec(memory_space=pltpu.SMEM)] + [ANY] * 8,
+        in_specs=[ANY] * 9,
         out_specs=(VM,) * 4,
         scratch_shapes=[
             vm((T, 2 * HD)), vm((T, 2 * HD)), vm((T, 2 * HD)), vm((T, HD)), vm((T, 2 * HD)),
@@ -711,9 +712,9 @@
             vm((2 * BF, D)), vm((2 * BF, D)), vm((2 * BF, CW)), vm((D, 2 * BF)), vm((D, 2 * BF)),
             vm((2, 4, 2, 4, 16, CW)),
             vm((KW, 8, HD), F32), vm((5, 8, HD), F32), vm((2, 4, 5, 8, HD), F32), vm((8, 5, 8, HD), F32),
-            vm((KW, D), F32), *buffers,
-            dma((8,)), dma((8,)), dma((NC,)), dma(()), dma((2,)), dma((6,)), dma((7,)), dma((7,)),
-            dma((NP,)), dma((NP * 3,)), dma((2 * NP,)), dma((2 * NP,)), dma((NP,)), dma((NP,)),
+            vm((KW, D), F32), pltpu.SMEM((1,), jnp.int32), *buffers,
+            dma(()), dma((8,)), dma((NC,)), dma(()), dma((2,)), dma((6,)), dma((2,)), dma((7,)),
+            dma(()), dma((len(RINGS) * 3,)), dma((2,)), dma((2 * NP,)), dma(()), dma((NP,)),
             dma((3,)), dma((3,)),
         ],
         compiler_params=pltpu.CompilerParams(

time: 84 us -> 82.7 us (0.985)
  Pallas kernels: 82.6 us -> 81.3 us
    pallas_call x1, Pallas kernels: 81.7 us -> 80.4 us  [backward(): pl.pallas_call(backward_kernel, out_shape=tuple((pltpu.VMEM(o.shape, o.dt...]
where the time goes in v7:
time: 82.7 us; the launch traced here: 82.6 us
  Pallas kernels  81.3 us (98%)
  between operations  1.29 us (2%)
    pallas_call x1, Pallas kernels, backward(): pl.pallas_call(backward_kernel, out_shape=tuple((pltpu.VMEM(o.shape, o.dt...  80.4 us

profile of v7, /device:TPU:1, one launch (start us, length us, event | category | flops | bytes accessed | tf_op | source)
XLA Modules:
  0.0 82.6 jit_solution(9070566637516940158)
XLA Ops:
  1.3 80.4 %shard_map.120 = (bf16[256,1024]{1,0:T(8,128)(2,1)S(1)}, f32[8,3072]{1,0:T(8,128)S(1)}, f32[8,1024]{1,0:T(8,128)S(1)}, f32[9,1024]{1,0:T(8,128)S(1)}) custom-call(s32[1]{0:T(128)S(6)} %copy.13.len_hbm, bf16[256,1024]{1,0:T(8,128)(2,1)} %bitcast.6, bf16[256,1024]{1,0:T(8,128)(2,1)} %bitcast.7, bf16[256,1024]{1,0:T(8,128)(2,1)} %bitcast.8, ...), custom_call_target="tpu_custom_call" | custom-call | tf_op jit(solution)/shard_map/pallas_call | solution.py:700
  81.7 0.9 %shard_map.121 = (bf16[256,1024]{1,0:T(8,128)(2,1)}, f32[8,3072]{1,0:T(8,128)}, f32[8,1024]{1,0:T(8,128)}, f32[9,1024]{1,0:T(8,128)}) custom-call(bf16[256,1024]{1,0:T(8,128)(2,1)S(1)} %get-tuple-element.12.refs_0_, f32[8,3072]{1,0:T(8,128)S(1)} %get-tuple-element.13.refs_1_, f32[8,1024]{1,0:T(8,128)S(1)} %get-tuple-element.14.refs_2_, ...), custom_call_target="tpu_custom_call" | custom-call | tf_op jit(solution)/shard_map/pallas_call | solution.py:725

commit v8 on v7

--- a/solution.py
+++ b/solution.py
@@ -43,13 +43,13 @@
 PARTS = (
     (0, 512, ("x", "y", "z")),
     (512, 512, ("x", "z", "y")),
-    (1024, 256, ("y", "x", "z")),
-    (1280, 256, ("z", "x", "y")),
-    (1536, 128, ("x", "y", "z")),
-    (1664, 128, ("y", "x", "z")),
-    (1792, 256, ("z", "y", "x")),
+    (1024, 256, ("y", "z", "x")),
+    (1280, 256, ("z", "y", "x")),
+    (1536, 256, ("x", "y", "z")),
+    (1792, 128, ("y", "x", "z")),
+    (1920, 128, ("z", "x", "y")),
 )
-RINGS = (0, 1, 2, 3)
+RINGS = (0, 1, 2, 3, 4)
 NP = len(PARTS)
 
 
@@ -606,13 +606,12 @@
 
         remote(BK, j * 2 + 1).start()
 
-    lax.fori_loop(0, 2, lambda j, c: (d_key(j), c)[1], 0)
+    lax.fori_loop(0, NC // 2, lambda j, c: (d_key(j), c)[1], 0)
+    local(BK).start()
     back(BV, VAL)
     rings[0][0].relay()
     weight(VAL)
     rings[1][0].begin()
-    lax.fori_loop(2, NC // 2, lambda j, c: (d_key(j), c)[1], 0)
-    local(BK).start()
     back(BQ, QUE)
     lax.fori_loop(0, D // BF, lambda n, c: (taps(n), c)[1], 0)
     swap_taps.start()
@@ -634,19 +633,20 @@
     lax.fori_loop(2, 4, d_input, 0)
     on(1, 0)
     taps_on(1, "y", taps_sum(0))
+    rings[4][0].relay()
     on(2, 0)
     on(3, 0)
     on(5, 0)
+    on(6, 0)
     on(4, 0)
-    on(6, 0)
     on(0, 1)
+    on(5, 1)
+    on(6, 1)
     on(2, 1)
     on(3, 1)
-    on(5, 1)
     on(1, 1)
     taps_last("z", taps_sum(1))
     on(4, 1)
-    on(6, 1)
     whole(att2.at[pl.ds(0, 32), :], halo_send)
     drain(send_sem, 8 * (NC - 1) * BF * HD * 2)
     drain(core_send.at[0], 4 * BF * D * 2)
@@ -658,7 +658,7 @@
     drain(ring_send, 3 * BF * ring_width * 2)
     drain(step_send.at[0], 3 * BF * (CW - ring_width) * 2)
     drain(step_send.at[1], 3 * BF // 4 * CW * 2)
-    for p in (0, 2, 3, 5, 1, 4, 6):
+    for p in (0, 5, 6, 2, 3, 1, 4):
         rings[p][2].end()
     taps_end()
     whole(do_in.at[pl.ds(0, 7 * 8 * (CW + 2 * HD) * 2 // (2 * HD)), :], last_send)

time: 82.7 us -> 82.7 us (level)
  no operation moved by 1% of the time
where the time goes in v8:
time: 82.7 us; the launch traced here: 82.6 us
  Pallas kernels  81.3 us (98%)
  between operations  1.29 us (2%)
    pallas_call x1, Pallas kernels, backward(): pl.pallas_call(backward_kernel, out_shape=tuple((pltpu.VMEM(o.shape, o.dt...  80.4 us

profile of v8, /device:TPU:1, one launch (start us, length us, event | category | flops | bytes accessed | tf_op | source)
XLA Modules:
  0.0 82.6 jit_solution(5202788064219071702)
XLA Ops:
  1.3 80.4 %shard_map.120 = (bf16[256,1024]{1,0:T(8,128)(2,1)S(1)}, f32[8,3072]{1,0:T(8,128)S(1)}, f32[8,1024]{1,0:T(8,128)S(1)}, f32[9,1024]{1,0:T(8,128)S(1)}) custom-call(s32[1]{0:T(128)S(6)} %copy.13.len_hbm, bf16[256,1024]{1,0:T(8,128)(2,1)} %bitcast.6, bf16[256,1024]{1,0:T(8,128)(2,1)} %bitcast.7, bf16[256,1024]{1,0:T(8,128)(2,1)} %bitcast.8, ...), custom_call_target="tpu_custom_call" | custom-call | tf_op jit(solution)/shard_map/pallas_call | solution.py:700
  81.7 0.9 %shard_map.121 = (bf16[256,1024]{1,0:T(8,128)(2,1)}, f32[8,3072]{1,0:T(8,128)}, f32[8,1024]{1,0:T(8,128)}, f32[9,1024]{1,0:T(8,128)}) custom-call(bf16[256,1024]{1,0:T(8,128)(2,1)S(1)} %get-tuple-element.12.refs_0_, f32[8,3072]{1,0:T(8,128)S(1)} %get-tuple-element.13.refs_1_, f32[8,1024]{1,0:T(8,128)S(1)} %get-tuple-element.14.refs_2_, ...), custom_call_target="tpu_custom_call" | custom-call | tf_op jit(solution)/shard_map/pallas_call | solution.py:725

commit v9 on v8

--- a/solution.py
+++ b/solution.py
@@ -49,6 +49,7 @@
     (1792, 128, ("y", "x", "z")),
     (1920, 128, ("z", "x", "y")),
 )
+PLANE = 4
 RINGS = (0, 1, 2, 3, 4)
 NP = len(PARTS)
 
@@ -64,7 +65,7 @@
     bufs = rest[: NP * 6]
     (send_sem, recv_sem, q_recv, halo_send, halo_recv, local_sem, core_send, core_recv,
      ring_send, ring_recv, step_send, step_recv, last_send, last_recv,
-     taps_send, taps_recv) = rest[NP * 6 :]
+     taps_send, taps_recv, plane_send, plane_recv) = rest[NP * 6 :]
     me = lax.axis_index("ctx")
     rec = lax.axis_index("rec")
     z, y = lax.div(me, 4), lax.rem(me, 4)
@@ -142,6 +143,47 @@
 
         lax.fori_loop(0, NC, step, 0)
 
+    core = lax.rem(rec, 2)
+    other = 1 - core
+    at = {"x": lax.rem(lax.div(rec, 2), 4), "y": y, "z": lax.div(rec, 8) * 2 + z}
+
+    def device(moved, to, on_core=core):
+        p = {**at, **({moved: to} if moved else {})}
+        return (
+            lax.rem(p["z"], 2) * 4 + p["y"],
+            lax.div(p["z"], 2) * 8 + p["x"] * 2 + on_core,
+        )
+
+    def off(axis, by):
+        return lax.rem(at[axis] + by, 4)
+
+    partner = device(None, None, other)
+    far = lax.rem(lax.div(rec, 8) + 1, 2)
+    greet = [partner] + [device("x", off("x", by)) for by in (1, 2, 3)]
+    greet += [device("z", far * 2 + zl) for zl in (0, 1)]
+    greet += [device(a, off(a, by), other) for a in "xyz" for by in (1, 2, 3)]
+
+    def on_plane(chip_z, by, on_core):
+        return (
+            lax.rem(chip_z, 2) * 4 + off("y", by),
+            lax.div(chip_z, 2) * 8 + at["x"] * 2 + on_core,
+        )
+
+    greet += [
+        on_plane(chip_z, by, on_core)
+        for by in (1, 2, 3)
+        for chip_z, on_core in (
+            (lax.div(rec, 8) * 2 + 1 - z, other),
+            *((far * 2 + zl, c) for zl in (0, 1) for c in (core, other)),
+        )
+    ]
+
+    barrier = pltpu.get_barrier_semaphore()
+    each_peer(
+        lambda d: pl.semaphore_signal(barrier, inc=1, device_id=(peer(d), rec), device_id_type=MESH)
+    )
+    for who in greet:
+        pl.semaphore_signal(barrier, inc=1, device_id=who, device_id_type=MESH)
     get_g = pltpu.make_async_copy(g_ref, g_vm, local_sem.at[0])
     get_w = pltpu.make_async_copy(wout_ref, wout_vm, local_sem.at[1])
     get_g.start()
@@ -157,32 +199,6 @@
     get_len = pltpu.make_async_copy(len_hbm, len_ref, local_sem.at[4])
     get_len.start()
 
-    core = lax.rem(rec, 2)
-    other = 1 - core
-    at = {"x": lax.rem(lax.div(rec, 2), 4), "y": y, "z": lax.div(rec, 8) * 2 + z}
-
-    def device(moved, to, on_core=core):
-        p = {**at, **({moved: to} if moved else {})}
-        return (
-            lax.rem(p["z"], 2) * 4 + p["y"],
-            lax.div(p["z"], 2) * 8 + p["x"] * 2 + on_core,
-        )
-
-    def off(axis, by):
-        return lax.rem(at[axis] + by, 4)
-
-    partner = device(None, None, other)
-    far = lax.rem(lax.div(rec, 8) + 1, 2)
-    greet = [partner] + [device("x", off("x", by)) for by in (1, 2, 3)]
-    greet += [device("z", far * 2 + zl) for zl in (0, 1)]
-    greet += [device(a, off(a, by), other) for a in "xyz" for by in (1, 2, 3)]
-
-    barrier = pltpu.get_barrier_semaphore()
-    each_peer(
-        lambda d: pl.semaphore_signal(barrier, inc=1, device_id=(peer(d), rec), device_id_type=MESH)
-    )
-    for who in greet:
-        pl.semaphore_signal(barrier, inc=1, device_id=who, device_id_type=MESH)
     pl.semaphore_wait(barrier, NC - 1 + len(greet))
 
     right, left = lax.rem(me + 1, NC), lax.rem(me + NC - 1, NC)
@@ -385,6 +401,29 @@
             zl, fixed.get("y", slice(None)), zh, fixed.get("x", slice(None)), :, pl.ds(start, width)
         ]
 
+    def by_core(total):
+        blocks = []
+        for c in (0, 1):
+            rows = total[..., c * 8 : c * 8 + 8, :]
+            h = rows.shape[-1] // 2
+            if h >= HD:
+                rows = jnp.concatenate([rows[..., :h], rows[..., h:]], axis=-2).astype(BF16)
+            blocks.append(rows)
+        return jnp.stack(blocks, axis=-3)
+
+    def put_out(part, parts_of):
+        start, width, _ = PARTS[part]
+        n, inside = divmod(start, HALF)
+        out, base = ((dwo_out, 0), (dwq_out, 2 * D), (dwq_out, 0), (dwq_out, D))[n]
+        for who, block in zip((core, other), parts_of):
+            first = base + who * HALF + inside
+            if width > HD:
+                h = width // 2
+                out[:, pl.ds(mult(first, HD), h)] = block[:8]
+                out[:, pl.ds(mult(first + h, HD), h)] = block[8:]
+            else:
+                out[:, pl.ds(mult(first, HD), HD)] = block
+
     class Stage:
         def __init__(self, part, stage):
             self.start, self.width, order = PARTS[part]
@@ -405,16 +444,12 @@
             )
 
         def keep(self, total):
-            if self.stage == 0:
+            if self.part == PLANE:
+                bufs[self.part * 6 + 4][...] = by_core(total)
+            elif self.stage == 0:
                 self.piece(0)[...] = total.astype(BF16)
             else:
-                pair = bufs[self.part * 6 + 4]
-                for c in (0, 1):
-                    rows = total[..., c * 8 : c * 8 + 8, :]
-                    if self.width > HD:
-                        h = self.width // 2
-                        rows = jnp.concatenate([rows[..., :h], rows[..., h:]], axis=-2)
-                    pair[..., c, :, :] = rows.astype(pair.dtype)
+                bufs[self.part * 6 + 4][...] = by_core(total)
 
     class Ring(Stage):
         def __init__(self, part):
@@ -504,22 +539,50 @@
             whole(self.buf, self.recv)
             b = [self.buf[n].astype(F32) for n in range(7)]
             here = self.rows(0, core)[...].astype(F32)
-            n, inside = divmod(self.start, HALF)
-            out, base = ((dwo_out, 0), (dwq_out, 2 * D), (dwq_out, 0), (dwq_out, D))[n]
-            for who, block in (
-                (core, (here + b[0]) + (b[1] + b[2])),
-                (other, (b[3] + b[4]) + (b[5] + b[6])),
-            ):
-                first = base + who * HALF + inside
-                if self.width > HD:
-                    h = self.width // 2
-                    out[:, pl.ds(mult(first, HD), h)] = block[:8]
-                    out[:, pl.ds(mult(first + h, HD), h)] = block[8:]
-                else:
-                    out[:, pl.ds(mult(first, HD), HD)] = block
+            put_out(
+                self.part,
+                ((here + b[0]) + (b[1] + b[2]), (b[3] + b[4]) + (b[5] + b[6])),
+            )
+
+    class Plane(Stage):
+        def __init__(self, part):
+            super().__init__(part, 1)
+            self.pair, self.buf = bufs[part * 6 + 4 : part * 6 + 6]
+            self.copies = []
+            moves = [(t, dz, dy) for t in (0, 1) for dz in range(4) for dy in range(4)]
+            for n, (turned, dz, dy) in enumerate(moves[1:]):
+                to = lax.rem(core + turned, 2)
+                self.copies.append(
+                    pltpu.make_async_remote_copy(
+                        src_ref=self.rows(dz, dy, to), dst_ref=self.buf.at[n],
+                        send_sem=plane_send, recv_sem=plane_recv,
+                        device_id=on_plane(off("z", dz), dy, to), device_id_type=MESH,
+                    )
+                )
+
+        def rows(self, dz, dy, to):
+            chip = off("z", dz)
+            return self.pair.at[lax.rem(chip, 2), off("y", dy), lax.div(chip, 2), to]
+
+        def begin(self):
+            for c in self.copies:
+                c.start()
+
+        def end(self):
+            whole(self.buf, plane_recv)
+            mine_sum = self.rows(0, 0, core)[...].astype(F32)
+            for n in range(15):
+                mine_sum = mine_sum + self.buf[n].astype(F32)
+            their_sum = self.buf[15].astype(F32)
+            for n in range(16, 31):
+                their_sum = their_sum + self.buf[n].astype(F32)
+            put_out(self.part, (mine_sum, their_sum))
 
     rings = [
-        (Ring(p) if p in RINGS else Direct(p, 0), Direct(p, 1), Last(p)) for p in range(NP)
+        (Ring(p), Plane(p))
+        if p == PLANE
+        else (Ring(p) if p in RINGS else Direct(p, 0), Direct(p, 1), Last(p))
+        for p in range(NP)
     ]
 
     def on(p, stage):
@@ -583,17 +646,17 @@
         din_vm[:, cols] = dot_nt(dqkv[...], wqkv_vm[cols, :]).astype(BF16)
         return carry
 
-    lax.fori_loop(0, 3, lambda d, c: (d_query(d), c)[1], 0)
+    lax.fori_loop(0, 2, lambda d, c: (d_query(d), c)[1], 0)
     arrived(BA)
     swap_att.start()
-    lax.fori_loop(3, 5, lambda d, c: (d_query(d), c)[1], 0)
+    lax.fori_loop(2, 4, lambda d, c: (d_query(d), c)[1], 0)
 
     swap_half(OUT).wait_recv()
     swap_att.wait_recv()
     turn_in(att2, att_t)
     product(att_t, OUT * HALF, HALF)
     rings[0][0].begin()
-    lax.fori_loop(5, NC, lambda d, c: (d_query(d), c)[1], 0)
+    lax.fori_loop(4, NC, lambda d, c: (d_query(d), c)[1], 0)
     local(BQ).start()
 
     def d_key(j):
@@ -606,10 +669,11 @@
 
         remote(BK, j * 2 + 1).start()
 
-    lax.fori_loop(0, NC // 2, lambda j, c: (d_key(j), c)[1], 0)
-    local(BK).start()
+    lax.fori_loop(0, 2, lambda j, c: (d_key(j), c)[1], 0)
     back(BV, VAL)
     rings[0][0].relay()
+    lax.fori_loop(2, NC // 2, lambda j, c: (d_key(j), c)[1], 0)
+    local(BK).start()
     weight(VAL)
     rings[1][0].begin()
     back(BQ, QUE)
@@ -621,32 +685,34 @@
     swap_taps.wait_recv()
     taps_on(0, "x", taps_c[pl.ds(core * 4, 5)] + taps_p[...])
     get_wq.wait()
+    rings[1][0].relay()
     back(BK, KEY)
     lax.fori_loop(0, 2, d_input, 0)
-    rings[1][0].relay()
+    swap_half(KEY).wait_recv()
+    product(li_t, KEY * HALF, HALF // 2)
+    rings[4][0].begin()
     rings[2][0].relay()
     rings[3][0].relay()
-    weight(KEY)
-    for p in (5, 6, 4):
-        rings[p][0].begin()
+    product(li_t, KEY * HALF + HALF // 2, HALF // 2)
+    rings[5][0].begin()
+    rings[6][0].begin()
+    taps_on(1, "y", taps_sum(0))
     on(0, 0)
     lax.fori_loop(2, 4, d_input, 0)
     on(1, 0)
-    taps_on(1, "y", taps_sum(0))
     rings[4][0].relay()
     on(2, 0)
     on(3, 0)
     on(5, 0)
     on(6, 0)
+    taps_last("z", taps_sum(1))
+    on(0, 1)
     on(4, 0)
-    on(0, 1)
     on(5, 1)
     on(6, 1)
+    on(1, 1)
     on(2, 1)
     on(3, 1)
-    on(1, 1)
-    taps_last("z", taps_sum(1))
-    on(4, 1)
     whole(att2.at[pl.ds(0, 32), :], halo_send)
     drain(send_sem, 8 * (NC - 1) * BF * HD * 2)
     drain(core_send.at[0], 4 * BF * D * 2)
@@ -657,11 +723,16 @@
     ring_width = sum(PARTS[p][1] for p in RINGS)
     drain(ring_send, 3 * BF * ring_width * 2)
     drain(step_send.at[0], 3 * BF * (CW - ring_width) * 2)
-    drain(step_send.at[1], 3 * BF // 4 * CW * 2)
-    for p in (0, 5, 6, 2, 3, 1, 4):
+    rows = 3 * BF // 4 * (CW - PARTS[PLANE][1]) * 2 // (4 * HD)
+    whole(q_aug.at[pl.ds(0, rows), :], step_send.at[1])
+    for p in (0, 5, 6, 1):
+        rings[p][2].end()
+    rings[4][1].end()
+    for p in (2, 3):
         rings[p][2].end()
     taps_end()
-    whole(do_in.at[pl.ds(0, 7 * 8 * (CW + 2 * HD) * 2 // (2 * HD)), :], last_send)
+    whole(do_in.at[pl.ds(0, 7 * 8 * CW * 2 // (2 * HD)), :], last_send)
+    whole(do_in.at[pl.ds(0, 31 * 16), :], plane_send)
 
 
 def collect_kernel(*refs):
@@ -688,8 +759,9 @@
         buffers += [vm(shape) for shape in (*halves, (sides, *leads[0], 16, width))]
         buffers.append(vm((3, *leads[1], 16, width)))
         block, kind = ((16, width // 2), BF16) if width > HD else ((8, width), F32)
-        buffers.append(vm((*leads[1], 2, *block), kind))
-        buffers.append(vm((7, *block), kind))
+        lead, count = (leads[0], 31) if p == PLANE else (leads[1], 7)
+        buffers.append(vm((*lead, 2, *block), kind))
+        buffers.append(vm((count, *block), kind))
     dma = pltpu.SemaphoreType.DMA
     outs = (
         jax.ShapeDtypeStruct((BF, D), BF16),
@@ -715,7 +787,7 @@
             vm((KW, D), F32), pltpu.SMEM((1,), jnp.int32), *buffers,
             dma(()), dma((8,)), dma((NC,)), dma(()), dma((2,)), dma((6,)), dma((2,)), dma((7,)),
             dma(()), dma((len(RINGS) * 3,)), dma((2,)), dma((2 * NP,)), dma(()), dma((NP,)),
-            dma((3,)), dma((3,)),
+            dma((3,)), dma((3,)), dma(()), dma(()),
         ],
         compiler_params=pltpu.CompilerParams(
             collective_id=0, has_side_effects=True, vmem_limit_bytes=60 * 1024 * 1024

time: 82.7 us -> 81 us (0.979)
  Pallas kernels: 81.3 us -> 79.6 us
    pallas_call x1, Pallas kernels: 80.4 us -> 78.7 us  [backward(): pl.pallas_call(backward_kernel, out_shape=tuple((pltpu.VMEM(o.shape, o.dt...]
where the time goes in v9:
time: 81 us; the launch traced here: 80.9 us
  Pallas kernels  79.6 us (98%)
  between operations  1.29 us (2%)
    pallas_call x1, Pallas kernels, backward(): pl.pallas_call(backward_kernel, out_shape=tuple((pltpu.VMEM(o.shape, o.dt...  78.7 us

profile of v9, /device:TPU:1, one launch (start us, length us, event | category | flops | bytes accessed | tf_op | source)
XLA Modules:
  0.0 80.9 jit_solution(7557853768472248815)
XLA Ops:
  1.3 78.7 %shard_map.120 = (bf16[256,1024]{1,0:T(8,128)(2,1)S(1)}, f32[8,3072]{1,0:T(8,128)S(1)}, f32[8,1024]{1,0:T(8,128)S(1)}, f32[9,1024]{1,0:T(8,128)S(1)}) custom-call(s32[1]{0:T(128)S(6)} %copy.13.len_hbm, bf16[256,1024]{1,0:T(8,128)(2,1)} %bitcast.6, bf16[256,1024]{1,0:T(8,128)(2,1)} %bitcast.7, bf16[256,1024]{1,0:T(8,128)(2,1)} %bitcast.8, ...), custom_call_target="tpu_custom_call" | custom-call | tf_op jit(solution)/shard_map/pallas_call | solution.py:772
  80.0 0.9 %shard_map.121 = (bf16[256,1024]{1,0:T(8,128)(2,1)}, f32[8,3072]{1,0:T(8,128)}, f32[8,1024]{1,0:T(8,128)}, f32[9,1024]{1,0:T(8,128)}) custom-call(bf16[256,1024]{1,0:T(8,128)(2,1)S(1)} %get-tuple-element.12.refs_0_, f32[8,3072]{1,0:T(8,128)S(1)} %get-tuple-element.13.refs_1_, f32[8,1024]{1,0:T(8,128)S(1)} %get-tuple-element.14.refs_2_, ...), custom_call_target="tpu_custom_call" | custom-call | tf_op jit(solution)/shard_map/pallas_call | solution.py:797

commit v10 on v9

--- a/solution.py
+++ b/solution.py
@@ -44,7 +44,7 @@
     (0, 512, ("x", "y", "z")),
     (512, 512, ("x", "z", "y")),
     (1024, 256, ("y", "z", "x")),
-    (1280, 256, ("z", "y", "x")),
+    (1280, 256, ("z", "x", "y")),
     (1536, 256, ("x", "y", "z")),
     (1792, 128, ("y", "x", "z")),
     (1920, 128, ("z", "x", "y")),

time: 81 us -> 81.1 us (level)
  no operation moved by 1% of the time
where the time goes in v10:
time: 81.1 us; the launch traced here: 81 us
  Pallas kernels  79.7 us (98%)
  between operations  1.29 us (2%)
    pallas_call x1, Pallas kernels, backward(): pl.pallas_call(backward_kernel, out_shape=tuple((pltpu.VMEM(o.shape, o.dt...  78.8 us

profile of v10, /device:TPU:1, one launch (start us, length us, event | category | flops | bytes accessed | tf_op | source)
XLA Modules:
  0.0 81.0 jit_solution(18092082733439400755)
XLA Ops:
  1.3 78.8 %shard_map.120 = (bf16[256,1024]{1,0:T(8,128)(2,1)S(1)}, f32[8,3072]{1,0:T(8,128)S(1)}, f32[8,1024]{1,0:T(8,128)S(1)}, f32[9,1024]{1,0:T(8,128)S(1)}) custom-call(s32[1]{0:T(128)S(6)} %copy.13.len_hbm, bf16[256,1024]{1,0:T(8,128)(2,1)} %bitcast.6, bf16[256,1024]{1,0:T(8,128)(2,1)} %bitcast.7, bf16[256,1024]{1,0:T(8,128)(2,1)} %bitcast.8, ...), custom_call_target="tpu_custom_call" | custom-call | tf_op jit(solution)/shard_map/pallas_call | solution.py:772
  80.1 0.9 %shard_map.121 = (bf16[256,1024]{1,0:T(8,128)(2,1)}, f32[8,3072]{1,0:T(8,128)}, f32[8,1024]{1,0:T(8,128)}, f32[9,1024]{1,0:T(8,128)}) custom-call(bf16[256,1024]{1,0:T(8,128)(2,1)S(1)} %get-tuple-element.12.refs_0_, f32[8,3072]{1,0:T(8,128)S(1)} %get-tuple-element.13.refs_1_, f32[8,1024]{1,0:T(8,128)S(1)} %get-tuple-element.14.refs_2_, ...), custom_call_target="tpu_custom_call" | custom-call | tf_op jit(solution)/shard_map/pallas_call | solution.py:797

commit v11 on v10

--- a/solution.py
+++ b/solution.py
@@ -687,7 +687,7 @@
     get_wq.wait()
     rings[1][0].relay()
     back(BK, KEY)
-    lax.fori_loop(0, 2, d_input, 0)
+    lax.fori_loop(0, 1, d_input, 0)
     swap_half(KEY).wait_recv()
     product(li_t, KEY * HALF, HALF // 2)
     rings[4][0].begin()
@@ -698,7 +698,7 @@
     rings[6][0].begin()
     taps_on(1, "y", taps_sum(0))
     on(0, 0)
-    lax.fori_loop(2, 4, d_input, 0)
+    lax.fori_loop(1, 4, d_input, 0)
     on(1, 0)
     rings[4][0].relay()
     on(2, 0)

time: 81.1 us -> 81.2 us (level)
  no operation moved by 1% of the time
where the time goes in v11:
time: 81.2 us; the launch traced here: 81.1 us
  Pallas kernels  79.8 us (98%)
  between operations  1.29 us (2%)
    pallas_call x1, Pallas kernels, backward(): pl.pallas_call(backward_kernel, out_shape=tuple((pltpu.VMEM(o.shape, o.dt...  78.9 us

profile of v11, /device:TPU:1, one launch (start us, length us, event | category | flops | bytes accessed | tf_op | source)
XLA Modules:
  0.0 81.1 jit_solution(14022407113509078795)
XLA Ops:
  1.3 78.9 %shard_map.120 = (bf16[256,1024]{1,0:T(8,128)(2,1)S(1)}, f32[8,3072]{1,0:T(8,128)S(1)}, f32[8,1024]{1,0:T(8,128)S(1)}, f32[9,1024]{1,0:T(8,128)S(1)}) custom-call(s32[1]{0:T(128)S(6)} %copy.13.len_hbm, bf16[256,1024]{1,0:T(8,128)(2,1)} %bitcast.6, bf16[256,1024]{1,0:T(8,128)(2,1)} %bitcast.7, bf16[256,1024]{1,0:T(8,128)(2,1)} %bitcast.8, ...), custom_call_target="tpu_custom_call" | custom-call | tf_op jit(solution)/shard_map/pallas_call | solution.py:772
  80.2 0.9 %shard_map.121 = (bf16[256,1024]{1,0:T(8,128)(2,1)}, f32[8,3072]{1,0:T(8,128)}, f32[8,1024]{1,0:T(8,128)}, f32[9,1024]{1,0:T(8,128)}) custom-call(bf16[256,1024]{1,0:T(8,128)(2,1)S(1)} %get-tuple-element.12.refs_0_, f32[8,3072]{1,0:T(8,128)S(1)} %get-tuple-element.13.refs_1_, f32[8,1024]{1,0:T(8,128)S(1)} %get-tuple-element.14.refs_2_, ...), custom_call_target="tpu_custom_call" | custom-call | tf_op jit(solution)/shard_map/pallas_call | solution.py:797
